TPU v7x, 32 devices: a whole 2x2x4 slice. The times are simulated.
32 devices in a mesh: dp: 16 (over z, y, core), mp: 2 (over x).
Axes of the slice: x: 2, y: 2, z: 4, core: 2. Of those that a mesh axis runs over, the one named last changes fastest.
Arguments:
- inputs: bfloat16 [16384, 768], P(('dp', 'mp')), may hold values from -6 to 6
- cotangent: bfloat16 [16384, 768], P(('dp', 'mp')), may hold values from -6 to 6
- w_query: bfloat16 [768, 768], replicated, may hold values from -0.21875 to 0.21875
- b_query: bfloat16 [768], replicated, may hold values from -3 to 3
- w_key: bfloat16 [768, 768], replicated, may hold values from -0.21875 to 0.21875
- b_key: bfloat16 [768], replicated, may hold values from -3 to 3
- w_value: bfloat16 [768, 768], replicated, may hold values from -0.21875 to 0.21875
- b_value: bfloat16 [768], replicated, may hold values from -3 to 3
- w_output: bfloat16 [768, 768], replicated, may hold values from -1.25 to 1.25
- b_output: bfloat16 [768], replicated, may hold values from -3 to 3
- norm1_gain: bfloat16 [768], replicated, may hold values from 0.5 to 1.5
- norm1_shift: bfloat16 [768], replicated, may hold values from -3 to 3
- w_inner: bfloat16 [768, 3072], P(None, 'mp'), may hold values from -0.21875 to 0.21875
- b_inner: bfloat16 [3072], P('mp'), may hold values from -3 to 3
- w_outer: bfloat16 [3072, 768], P('mp'), may hold values from -0.109375 to 0.109375
- b_outer: bfloat16 [768], replicated, may hold values from -3 to 3
- norm2_gain: bfloat16 [768], replicated, may hold values from 0.5 to 1.5
- norm2_shift: bfloat16 [768], replicated, may hold values from -3 to 3
- rel_table: bfloat16 [512, 768], replicated, may hold values from -6 to 6
- rel_gain: bfloat16 [768], replicated, may hold values from 0.5 to 1.5
- rel_shift: bfloat16 [768], replicated, may hold values from -3 to 3
- block_group: int32 [32], P(('dp', 'mp')), may hold values from 0 to 2, as said below
- seq_lengths: int32 [32, 4], P(('dp', 'mp')), may hold values from 0 to 512, as said below
Outputs:
- layer_out: float32 [16384, 768], P(('dp', 'mp'))
- input_grad: float32 [16384, 768], P(('dp', 'mp'))
- grad_w_query: float32 [768, 768], replicated
- grad_b_query: float32 [768], replicated
- grad_w_key: float32 [768, 768], replicated
- grad_b_key: float32 [768], replicated
- grad_w_value: float32 [768, 768], replicated
- grad_b_value: float32 [768], replicated
- grad_w_output: float32 [768, 768], replicated
- grad_b_output: float32 [768], replicated
- grad_norm1_gain: float32 [768], replicated
- grad_norm1_shift: float32 [768], replicated
- grad_w_inner: float32 [768, 3072], P(None, 'mp')
- grad_b_inner: float32 [3072], P('mp')
- grad_w_outer: float32 [3072, 768], P('mp')
- grad_b_outer: float32 [768], replicated
- grad_norm2_gain: float32 [768], replicated
- grad_norm2_shift: float32 [768], replicated
- grad_rel_table: float32 [512, 768], replicated
- grad_rel_gain: float32 [768], replicated
- grad_rel_shift: float32 [768], replicated
Inputs may be any that keep to these rules, and one draw needn't show every extreme that they name: `block_group`: A block of group 0 holds one sequence of up to 512 tokens, of group 1 two of up to 256, of group 2 four of up to 128. `seq_lengths`: entry s is the live length of the block's sequence s; entries past the group's sequences are 0; every sequence has at least a quarter of its places, and the first sequence of every block fills its places.
All inputs are finite; a program needn't handle non-finite values.
Results may differ from a plain program's by a relative error of at most 0.024.
Values may be sent and summed in bfloat16 or wider, within the bound.
No kernel may reach another device: no remote copies, remote signals or barrier semaphores. Data moves between devices by JAX's collectives and lax.ppermute only.
A program may use at most 256 MiB of HBM per device.

v0:
```python
import math

import jax
import jax.numpy as jnp
import numpy as np
from jax import lax
from jax.sharding import PartitionSpec as P

HEADS = 12


EPS = 1e-06
MAXIMAL_PRECISION = lax.Precision.HIGHEST


def bucket_line(half_rows):
    table_rows = 2 * half_rows
    middle = half_rows // 2
    relative = table_rows - 1 - np.arange(2 * table_rows - 1)
    signed = np.sign(relative)
    absolute = np.where((relative < middle) & (relative > -middle), middle - 1, np.abs(relative))
    log_place = (
        np.ceil(np.log(absolute / middle) / np.log((table_rows - 1) / middle) * (middle - 1))
        + middle
    )
    placed = np.where(absolute <= middle, relative, log_place * signed)
    return (placed + half_rows).astype(np.int32)


def layer_norm(array_in, gains, offsets):
    average = jnp.mean(array_in, axis=-1, keepdims=True)
    center = array_in - average
    variance = jnp.mean(center * center, axis=-1, keepdims=True)
    return center * lax.rsqrt(variance + EPS) * gains + offsets


def valid_pairs(group_kind, lengths, block_rows):
    capacity = jnp.right_shift(jnp.int32(block_rows), group_kind)
    places = jnp.arange(block_rows, dtype=jnp.int32)
    owner_slot = places // capacity
    offset = places - owner_slot * capacity
    slot_ids = jnp.arange(4, dtype=jnp.int32)
    limits = jnp.sum(
        jnp.where(owner_slot[:, None] == slot_ids[None, :], lengths[None, :], 0), axis=1
    )
    return (owner_slot[:, None] == owner_slot[None, :]) & (offset < limits)[None, :]


def skewed(line_scores):
    head_count, row_count, line_count = line_scores.shape
    padded = jnp.pad(line_scores, ((0, 0), (0, 0), (0, 1)))
    flat = padded.reshape(head_count, row_count * (line_count + 1))
    piece = flat[:, row_count - 1 : row_count - 1 + row_count * line_count]
    return piece.reshape(head_count, row_count, line_count)[:, :, :row_count]


def product(left, right):
    return jnp.dot(left, right, preferred_element_type=jnp.float32)


def product_nt(left, right):
    return lax.dot_general(
        left, right, (((1,), (1,)), ((), ())), preferred_element_type=jnp.float32
    )


def product_tn(left, right):
    return lax.dot_general(
        left, right, (((0,), (0,)), ((), ())), preferred_element_type=jnp.float32
    )


def col_sums(array_in):
    return jnp.sum(array_in.astype(jnp.float32), axis=0)


def exact_gelu(array_in):
    return jax.nn.gelu(array_in, approximate=False)


def as_float(array_in):
    return array_in.astype(jnp.float32)


def per_device(
    inputs,
    cotangent,
    w_query,
    b_query,
    w_key,
    b_key,
    w_value,
    b_value,
    w_output,
    b_output,
    norm1_gain,
    norm1_shift,
    w_inner,
    b_inner,
    w_outer,
    b_outer,
    norm2_gain,
    norm2_shift,
    rel_table,
    rel_gain,
    rel_shift,
    block_group,
    seq_lengths,
):
    rows_dev, model_width = inputs.shape
    head_count = HEADS
    head_size = model_width // head_count
    block_count = block_group.shape[0]
    block_rows = rows_dev // block_count
    line_forward = bucket_line(block_rows // 2)
    line_backward = line_forward[::-1].copy()
    onehot_forward = jnp.asarray(
        (line_forward[:, None] == np.arange(block_rows)[None, :]).astype(np.float32)
    )
    onehot_backward = jnp.asarray(
        (line_backward[:, None] == np.arange(block_rows)[None, :]).astype(np.float32)
    )
    score_scale = 1.0 / math.sqrt(3 * head_size)

    def combined(content, query_line, key_line):
        key_side = jnp.swapaxes(skewed(key_line), 1, 2)
        return (content + skewed(query_line) + key_side) * score_scale

    def project(left, weight, bias):
        return (product(left, weight) + as_float(bias)).astype(jnp.bfloat16)

    rel_normed, rel_pull = jax.vjp(
        layer_norm, as_float(rel_table), as_float(rel_gain), as_float(rel_shift)
    )
    rel_low = rel_normed.astype(jnp.bfloat16)
    position_key_rows = project(rel_low, w_key, b_key).reshape(block_rows, head_count, head_size)
    position_query_rows = project(rel_low, w_query, b_query).reshape(
        block_rows, head_count, head_size
    )
    key_line_rows = position_key_rows[jnp.asarray(line_forward)]
    query_line_rows = position_query_rows[jnp.asarray(line_backward)]
    query_heads = project(inputs, w_query, b_query).reshape(
        block_count, block_rows, head_count, head_size
    )
    key_heads = project(inputs, w_key, b_key).reshape(
        block_count, block_rows, head_count, head_size
    )
    value_heads = project(inputs, w_value, b_value).reshape(
        block_count, block_rows, head_count, head_size
    )

    def raw_scores(query_tile_block, key_tile_block):
        content = jnp.einsum(
            "ihd,jhd->hij", query_tile_block, key_tile_block, preferred_element_type=jnp.float32
        )
        query_line = jnp.einsum(
            "ihd,shd->his", query_tile_block, key_line_rows, preferred_element_type=jnp.float32
        )
        key_line = jnp.einsum(
            "jhd,shd->hjs", key_tile_block, query_line_rows, preferred_element_type=jnp.float32
        )
        return (content, query_line, key_line)

    number = 0
    content, query_line, key_line = raw_scores(query_heads[number], key_heads[number])
    valid_mask = valid_pairs(block_group[number], seq_lengths[number], block_rows)
    scores = jnp.where(valid_mask[None], combined(content, query_line, key_line), -1e30)
    row_top = jnp.max(scores, axis=2, keepdims=True)
    exp_scores = jnp.exp(scores - row_top)
    row_total = jnp.sum(exp_scores, axis=2, keepdims=True)
    att_probs = exp_scores / row_total
    log_totals = [row_top + jnp.log(row_total)]
    attended = jnp.einsum(
        "hij,jhd->ihd",
        att_probs.astype(jnp.bfloat16),
        value_heads[number],
        preferred_element_type=jnp.float32,
    )
    mixed_blocks = attended.reshape(block_rows, model_width)
    mixed_low = mixed_blocks.astype(jnp.bfloat16)
    residual = product(mixed_low, w_output) + as_float(b_output) + as_float(inputs)
    hidden, norm1_pull = jax.vjp(layer_norm, residual, as_float(norm1_gain), as_float(norm1_shift))
    hidden_low = hidden.astype(jnp.bfloat16)
    gathered = lax.all_gather(hidden_low, "mp", axis=0, tiled=True)
    inner_pre = product(gathered, w_inner) + as_float(b_inner)
    active, gelu_pull = jax.vjp(exact_gelu, inner_pre)
    active_low = active.astype(jnp.bfloat16)
    branch = lax.psum_scatter(
        product(active_low, w_outer), "mp", scatter_dimension=0, tiled=True
    ) + as_float(b_outer)
    layer_out, norm2_pull = jax.vjp(
        layer_norm, hidden + branch, as_float(norm2_gain), as_float(norm2_shift)
    )
    d_pre_two, grad_norm2_gain, grad_norm2_shift = norm2_pull(as_float(cotangent))
    branch_grad = d_pre_two.astype(jnp.bfloat16)
    grad_b_outer = col_sums(branch_grad)
    grad_gathered = lax.all_gather(branch_grad, "mp", axis=0, tiled=True)
    d_active = product_nt(grad_gathered, w_outer)
    d_inner = gelu_pull(d_active)[0].astype(jnp.bfloat16)
    grad_w_outer = product_tn(active_low, grad_gathered)
    grad_w_inner = product_tn(gathered, d_inner)
    grad_b_inner = col_sums(d_inner)
    d_hidden_ffn = lax.psum_scatter(
        product_nt(d_inner, w_inner), "mp", scatter_dimension=0, tiled=True
    )
    grad_w_inner, grad_b_inner, grad_w_outer = (
        lax.psum(grad_w_inner.astype(jnp.bfloat16), "dp").astype(jnp.float32),
        lax.psum(grad_b_inner.astype(jnp.bfloat16), "dp").astype(jnp.float32),
        lax.psum(grad_w_outer.astype(jnp.bfloat16), "dp").astype(jnp.float32),
    )
    d_residual, grad_norm1_gain, grad_norm1_shift = norm1_pull(d_pre_two + d_hidden_ffn)
    attn_grad = d_residual.astype(jnp.bfloat16)
    grad_b_output = col_sums(attn_grad)
    grad_w_output = product_tn(mixed_low, attn_grad)
    d_mixed = (
        product_nt(attn_grad, w_output)
        .astype(jnp.bfloat16)
        .reshape(block_count, block_rows, head_count, head_size)
    )
    pos_key_grad = jnp.zeros((block_rows, head_count, head_size), jnp.float32)
    pos_query_grad = jnp.zeros((block_rows, head_count, head_size), jnp.float32)
    number = 0
    query_tile_block = query_heads[number]
    key_tile_block = key_heads[number]
    v_block = value_heads[number]
    d_out = d_mixed[number]
    content, query_line, key_line = raw_scores(query_tile_block, key_tile_block)
    valid_mask = valid_pairs(block_group[number], seq_lengths[number], block_rows)
    scores = jnp.where(valid_mask[None], combined(content, query_line, key_line), -1e30)
    att_probs = jnp.where(valid_mask[None], jnp.exp(scores - log_totals[number]), 0.0)
    d_probs = jnp.einsum("ihd,jhd->hij", d_out, v_block, preferred_element_type=jnp.float32)
    d_value_blocks = jnp.einsum(
        "hij,ihd->jhd", att_probs.astype(jnp.bfloat16), d_out, preferred_element_type=jnp.float32
    ).astype(jnp.bfloat16)
    d_scores = att_probs * (d_probs - jnp.sum(att_probs * d_probs, axis=2, keepdims=True))
    unused_scores, score_pull = jax.vjp(combined, content, query_line, key_line)
    d_content, d_query_line, d_key_line = score_pull(d_scores)
    d_content = d_content.astype(jnp.bfloat16)
    query_position_gradient = jnp.einsum(
        "his,sm->him",
        d_query_line,
        onehot_forward,
        precision=MAXIMAL_PRECISION,
        preferred_element_type=jnp.float32,
    ).astype(jnp.bfloat16)
    key_position_gradient = jnp.einsum(
        "hjs,sm->hjm",
        d_key_line,
        onehot_backward,
        precision=MAXIMAL_PRECISION,
        preferred_element_type=jnp.float32,
    ).astype(jnp.bfloat16)
    d_query_block = jnp.einsum(
        "hij,jhd->ihd", d_content, key_tile_block, preferred_element_type=jnp.float32
    )
    d_query_block = d_query_block + jnp.einsum(
        "qjk,kqv->jqv",
        query_position_gradient,
        position_key_rows,
        preferred_element_type=jnp.float32,
    )
    d_key_block = jnp.einsum(
        "hij,ihd->jhd", d_content, query_tile_block, preferred_element_type=jnp.float32
    )
    d_key_block = d_key_block + jnp.einsum(
        "mpl,lmg->pmg",
        key_position_gradient,
        position_query_rows,
        preferred_element_type=jnp.float32,
    )
    d_query_blocks = [d_query_block.astype(jnp.bfloat16)]
    d_key_blocks = [d_key_block.astype(jnp.bfloat16)]
    pos_key_grad = pos_key_grad + jnp.einsum(
        "xbn,bxo->nxo",
        query_position_gradient,
        query_tile_block,
        preferred_element_type=jnp.float32,
    )
    pos_query_grad = pos_query_grad + jnp.einsum(
        "ogn,gou->nou", key_position_gradient, key_tile_block, preferred_element_type=jnp.float32
    )
    d_query = jnp.concatenate(d_query_blocks, axis=0).reshape(rows_dev, model_width)
    d_key = jnp.concatenate(d_key_blocks, axis=0).reshape(rows_dev, model_width)
    d_value = d_value_blocks.reshape(rows_dev, model_width)
    d_pos_key = pos_key_grad.reshape(block_rows, model_width).astype(jnp.bfloat16)
    d_pos_query = pos_query_grad.reshape(block_rows, model_width).astype(jnp.bfloat16)
    grad_w_query = product_tn(inputs, d_query) + product_tn(rel_low, d_pos_query)
    grad_b_query = col_sums(d_query) + col_sums(d_pos_query)
    grad_w_key = product_tn(inputs, d_key) + product_tn(rel_low, d_pos_key)
    grad_b_key = col_sums(d_key) + col_sums(d_pos_key)
    grad_w_value = product_tn(inputs, d_value)
    grad_b_value = col_sums(d_value)
    d_rel = product_nt(d_pos_key, w_key) + product_nt(d_pos_query, w_query)
    grad_rel_table, grad_rel_gain, grad_rel_shift = rel_pull(d_rel)
    input_grad = (
        d_residual
        + product_nt(d_query, w_query)
        + product_nt(d_key, w_key)
        + product_nt(d_value, w_value)
    )
    (
        grad_w_query,
        grad_b_query,
        grad_w_key,
        grad_b_key,
        grad_w_value,
        grad_b_value,
        grad_w_output,
        grad_b_output,
        grad_norm1_gain,
        grad_norm1_shift,
        grad_b_outer,
        grad_norm2_gain,
        grad_norm2_shift,
        grad_rel_table,
        grad_rel_gain,
        grad_rel_shift,
    ) = lax.psum(
        (
            grad_w_query,
            grad_b_query,
            grad_w_key,
            grad_b_key,
            grad_w_value,
            grad_b_value,
            grad_w_output,
            grad_b_output,
            grad_norm1_gain,
            grad_norm1_shift,
            grad_b_outer,
            grad_norm2_gain,
            grad_norm2_shift,
            grad_rel_table,
            grad_rel_gain,
            grad_rel_shift,
        ),
        ("dp", "mp"),
    )
    return (
        layer_out,
        input_grad,
        grad_w_query,
        grad_b_query,
        grad_w_key,
        grad_b_key,
        grad_w_value,
        grad_b_value,
        grad_w_output,
        grad_b_output,
        grad_norm1_gain,
        grad_norm1_shift,
        grad_w_inner,
        grad_b_inner,
        grad_w_outer,
        grad_b_outer,
        grad_norm2_gain,
        grad_norm2_shift,
        grad_rel_table,
        grad_rel_gain,
        grad_rel_shift,
    )


def solution(mesh):
    placed = (
        P(("dp", "mp"), None),
        P(("dp", "mp"), None),
        P(),
        P(),
        P(),
        P(),
        P(),
        P(),
        P(),
        P(),
        P(),
        P(),
        P(None, "mp"),
        P("mp"),
        P("mp", None),
        P(),
        P(),
        P(),
        P(),
        P(),
        P(),
        P(("dp", "mp")),
        P(("dp", "mp"), None),
    )
    return jax.shard_map(
        per_device,
        mesh=mesh,
        in_specs=placed,
        out_specs=(
            P(("dp", "mp"), None),
            P(("dp", "mp"), None),
            P(),
            P(),
            P(),
            P(),
            P(),
            P(),
            P(),
            P(),
            P(),
            P(),
            P(None, "mp"),
            P("mp"),
            P("mp", None),
            P(),
            P(),
            P(),
            P(),
            P(),
            P(),
        ),
        check_vma=False,
    )
```

profile of v0, /device:TPU:0, one launch (start us, length us, event | category | flops | bytes accessed | tf_op | source)
XLA Modules:
  0.0 1274.4 jit_solution(3377157581306931011)
XLA Ops:
  71.5 17.6 %pad.30 = f32[12,512,1024]{2,1,0:T(8,128)} pad(f32[12,512,1023]{2,1,0:T(8,128)} %fusion.36, f32[]{:T(128)} %constant.27.clone.1), padding=0_0x0_0x0_1 | pad | bytes 50307076 | tf_op jit(solution)/shard_map/jit(_pad)/pad | solution.py:51
  99.9 39.7 %copy.121 = f32[2,8,512,1024]{3,1,2,0:T(8,128)} copy(f32[2,8,512,1024]{3,2,1,0:T(8,128)S(1)} %bitcast.128) | data formatting | bytes 67108864
  139.7 25.5 %slice.26 = f32[12,523776]{1,0:T(8,128)} slice(f32[12,524288]{1,0:T(8,128)} %bitcast.131), slice={[0:12], [511:524287]} | slice | bytes 50282496 | tf_op jit(solution)/shard_map/slice | solution.py:53
  165.2 54.0 %reshape.292 = f32[12,512,1023]{2,1,0:T(8,128)} reshape(f32[12,523776]{1,0:T(8,128)} %slice.26) | data formatting | bytes 50282496 | tf_op jit(solution)/shard_map/reshape | solution.py:54
  265.1 17.6 %pad.31 = f32[12,512,1024]{2,1,0:T(8,128)} pad(f32[12,512,1023]{2,1,0:T(8,128)} %fusion.34, f32[]{:T(128)} %constant.27.clone.1), padding=0_0x0_0x0_1 | pad | bytes 50307076 | tf_op jit(solution)/shard_map/jit(_pad)/pad | solution.py:51
  293.5 39.7 %copy.122 = f32[2,8,512,1024]{3,1,2,0:T(8,128)} copy(f32[2,8,512,1024]{3,2,1,0:T(8,128)S(1)} %bitcast.129) | data formatting | bytes 67108864
  333.3 25.5 %slice.28 = f32[12,523776]{1,0:T(8,128)} slice(f32[12,524288]{1,0:T(8,128)} %bitcast.132), slice={[0:12], [511:524287]} | slice | bytes 50282496 | tf_op jit(solution)/shard_map/slice | solution.py:53
  358.8 41.7 %reshape.295 = f32[12,512,1023]{2,1,0:T(8,128)} reshape(f32[12,523776]{1,0:T(8,128)} %slice.28) | data formatting | bytes 50282496 | tf_op jit(solution)/shard_map/reshape | solution.py:54
  429.3 30.0 %all-gather.3.cloned.1.call-done = bf16[1024,768]{1,0:T(8,128)(2,1)} async-done(((bf16[512,768]{1,0:T(8,128)(2,1)}), bf16[1024,768]{1,0:T(8,128)(2,1)}) %all-gather.3.cloned.1.call-update) | async-done | bytes 1572880 | tf_op jit(solution)/shard_map/all_gather | solution.py:184
  459.3 18.3 %multiply_convert_fusion = (bf16[1024,1536]{1,0:T(8,128)(2,1)S(1)}, f32[1024,1536]{1,0:T(8,128)}, f32[1024,1536]{1,0:T(8,128)}) fusion(f32[1536]{0:T(1024)S(1)} %convert_element_type.218, bf16[1024,768]{1,0:T(8,128)(2,1)} %all-gather.3.cloned.1.call-done, bf16[768,1536]{1,0:T(8,128)(2,1)S(1)} %copy-done), kind=kOutput, calls=%fused_computation.27 | convolution fusion | flops 2519728128 | bytes 19666944 | tf_op jit(solution)/shard_map/dot_general | solution.py:58
  484.2 42.8 %reduce-scatter.3.cloned.1.call-done = f32[512,768]{1,0:T(8,128)} async-done(((f32[1024,768]{1,0:T(8,128)}), f32[512,768]{1,0:T(8,128)}) %reduce-scatter.3.cloned.1.call-update) | async-done | bytes 1572880 | tf_op jit(solution)/shard_map/reduce_scatter | solution.py:188
  535.9 27.3 %all-gather.5.cloned.1.call-done = bf16[1024,768]{1,0:T(8,128)(2,1)} async-done(((bf16[512,768]{1,0:T(8,128)(2,1)}), bf16[1024,768]{1,0:T(8,128)(2,1)}) %all-gather.5.cloned.1.call-update) | async-done | bytes 1572880 | tf_op jit(solution)/shard_map/all_gather | solution.py:197
  591.2 32.3 %reduce-scatter.5.cloned.1.call-done = f32[512,768]{1,0:T(8,128)} async-done(((f32[1024,768]{1,0:T(8,128)}), f32[512,768]{1,0:T(8,128)}) %reduce-scatter.5.cloned.1.call-update) | async-done | bytes 1572880 | tf_op jit(solution)/shard_map/reduce_scatter | solution.py:203
  697.6 38.7 %reshape.296 = f32[12,523776]{1,0:T(8,128)} reshape(f32[12,512,1023]{2,1,0:T(8,128)} %pad.32.clone) | data formatting | bytes 50282496 | tf_op jit(solution)/shard_map/transpose(jvp())/reshape | solution.py:54
  751.6 35.7 %copy.123 = f32[2,8,512,1024]{3,2,1,0:T(8,128)} copy(f32[2,8,512,1024]{3,1,2,0:T(8,128)S(1)} %bitcast.130) | data formatting | bytes 67108864
  787.3 17.7 %slice.30 = f32[12,512,1024]{2,1,0:T(8,128)} slice(f32[16,512,1024]{2,1,0:T(8,128)} %bitcast.133), slice={[0:12], [0:512], [0:1024]} | slice | bytes 50331648 | tf_op jit(solution)/shard_map/transpose(jvp())/reshape | solution.py:52
  805.1 44.2 %fusion.28 = bf16[12,512,512]{2,1,0:T(8,128)(2,1)S(1)} fusion(f32[1023,512,1]{1,0,2:T(8,128)S(1)} %copy-done.85, f32[12,512,1024]{2,1,0:T(8,128)} %slice.30), kind=kOutput, calls=%fused_computation.44 | convolution fusion | flops 38620102656 | bytes 33552384 | tf_op jit(solution)/shard_map/his,sm->him/dot_general | solution.py:239
  864.6 38.2 %reshape.299 = f32[12,523776]{1,0:T(8,128)} reshape(f32[12,512,1023]{2,1,0:T(8,128)} %pad.35) | data formatting | bytes 50282496 | tf_op jit(solution)/shard_map/transpose(jvp())/reshape | solution.py:54
  918.1 35.9 %copy.124 = f32[2,8,512,1024]{3,2,1,0:T(8,128)} copy(f32[2,8,512,1024]{3,1,2,0:T(8,128)S(1)} %bitcast.127) | data formatting | bytes 67108864
  954.0 17.7 %slice.31 = f32[12,512,1024]{2,1,0:T(8,128)} slice(f32[16,512,1024]{2,1,0:T(8,128)} %bitcast.134), slice={[0:12], [0:512], [0:1024]} | slice | bytes 50331648 | tf_op jit(solution)/shard_map/transpose(jvp())/reshape | solution.py:52
  971.8 44.3 %fusion.31 = bf16[12,512,512]{2,1,0:T(8,128)(2,1)S(1)} fusion(f32[1023,512,1]{1,0,2:T(8,128)S(1)} %copy-done.84, f32[12,512,1024]{2,1,0:T(8,128)} %slice.31), kind=kOutput, calls=%fused_computation.45 | convolution fusion | flops 38620102656 | bytes 33552384 | tf_op jit(solution)/shard_map/hjs,sm->hjm/dot_general | solution.py:246
  1031.9 34.3 %psum.144 = bf16[1536]{0:T(1024)(128)(2,1)S(1)} all-reduce(bf16[1536]{0:T(1024)(128)(2,1)S(1)} %copy-done.66), channel_id=1, replica_groups=mesh['dp'=16,'mp'=2] {'dp'}, use_global_device_ids=true, to_apply=%region_36.37 | all-reduce | flops 1536 | bytes 6144 | tf_op jit(solution)/shard_map/psum | solution.py:208
  1074.5 39.1 %all-reduce.6 = (f32[768]{0:T(1024)}, f32[768]{0:T(1024)}, f32[768]{0:T(1024)}, f32[768]{0:T(1024)}, f32[768]{0:T(1024)}, /*index=5*/f32[768]{0:T(1024)}, f32[76...) all-reduce(f32[768]{0:T(1024)S(1)} %add.287, ...), channel_id=1, replica_groups=mesh['dp'=16,'mp'=2] {'dp','mp'}, use_global_device_ids=true, to_apply=%region_19.20 | all-reduce | flops 8448 | bytes 67584 | tf_op jit(solution)/shard_map/psum | solution.py:318
  1119.3 135.4 %all-reduce.12.cloned.1.call-done = (f32[768,768]{0,1:T(8,128)}, f32[768,768]{0,1:T(8,128)}, f32[768,768]{0,1:T(8,128)}, f32[768,768]{1,0:T(8,128)}, f32[512,768]{1,0:T(8,128)}) async-done(((f32[768,768]{0,1:T(8,128)}, f32[768,768]{0,1:T(8,128)}, f32[768,768]{0,1:T(8,128)}, f32[768,768]{1,0:T(8,128)}, f32[512,768]{1,0:T(8,128)}), (f32[768,768]{0,1:T(8,128)}, f32[768,768]{0,1:T(8,128)}, ...) | async-done | bytes 11010064 | tf_op jit(solution)/shard_map/psum | solution.py:318
  (311 shorter events, 365.3 us)
Async XLA Ops:
  7.2 452.1 %copy-start = (bf16[768,1536]{1,0:T(8,128)(2,1)S(1)}, bf16[768,1536]{1,0:T(8,128)(2,1)}, u32[]{:S(2)}) copy-start(bf16[768,1536]{1,0:T(8,128)(2,1)} %param.39) | copy-start | bytes 7077892
  7.2 452.1 %all-gather.3.cloned.1.call-start = ((), (), s32[]{:S(2)}) async-start(), calls=%async_computation.2 | async-start | bytes 2359296 | tf_op jit(solution)/shard_map/all_gather | solution.py:184
  8.7 9.5 copy-start.46
  34.5 630.2 %copy-start.8 = (bf16[512,768]{0,1:T(8,128)(2,1)}, bf16[512,768]{0,1:T(8,128)(2,1)S(1)}, u32[]{:S(2)}) copy-start(bf16[512,768]{0,1:T(8,128)(2,1)S(1)} %copy.94) | copy-start | bytes 2359300
  358.8 41.7 %copy-start.37 = (pred[512,512]{0,1:T(8,128)(4,1)S(1)}, pred[512,512]{0,1:T(8,128)(4,1)}, u32[]{:S(2)}) copy-start(pred[512,512]{0,1:T(8,128)(4,1)} %compare_and_fusion) | copy-start | bytes 786436
  400.5 21.4 %copy-start.38 = (bf16[512,768]{0,1:T(8,128)(2,1)S(1)}, bf16[512,768]{0,1:T(8,128)(2,1)}, u32[]{:S(2)}) copy-start(bf16[512,768]{0,1:T(8,128)(2,1)} %copy.92) | copy-start | bytes 2359300
  415.3 8.2 copy-start.3
  429.3 97.8 %reduce-scatter.3.cloned.1.call-start = ((), (), s32[]{:S(2)}) async-start(), calls=%async_computation.3 | async-start | bytes 4718592 | tf_op jit(solution)/shard_map/reduce_scatter | solution.py:188
  459.3 19.9 %copy-start.77 = (bf16[1536,768]{1,0:T(8,128)(2,1)S(1)}, bf16[1536,768]{1,0:T(8,128)(2,1)}, u32[]{:S(2)}) copy-start(bf16[1536,768]{1,0:T(8,128)(2,1)} %param.41) | copy-start | bytes 7077892
  483.5 79.6 %all-gather.5.cloned.1.call-start = ((), (), s32[]{:S(2)}) async-start(), calls=%async_computation.4 | async-start | bytes 2359296 | tf_op jit(solution)/shard_map/all_gather | solution.py:197
  535.8 87.7 %reduce-scatter.5.cloned.1.call-start = ((), (), s32[]{:S(2)}) async-start(), calls=%async_computation.5 | async-start | bytes 4718592 | tf_op jit(solution)/shard_map/reduce_scatter | solution.py:203
  580.0 486.8 %all-reduce.14.cloned.1.call-start = ((), (), s32[]{:S(2)}) async-start(), calls=%async_computation.7 | async-start | bytes 9437184 | tf_op jit(solution)/shard_map/psum | solution.py:207
  590.8 32.7 %copy-start.5 = (f32[512,768]{1,0:T(8,128)S(1)}, f32[512,768]{1,0:T(8,128)}, u32[]{:S(2)}) copy-start(f32[512,768]{1,0:T(8,128)} %copy-done.4) | copy-start | bytes 4718596
  590.8 663.9 %all-reduce.12.cloned.1.call-start = ((), (), s32[]{:S(2)}) async-start(), calls=%async_computation.6 | async-start | bytes 22020096 | tf_op jit(solution)/shard_map/psum | solution.py:318
  641.0 39.8 %copy-start.22 = (bf16[12,64,512]{2,1,0:T(8,128)(2,1)}, bf16[12,64,512]{2,1,0:T(8,128)(2,1)S(1)}, u32[]{:S(2)}) copy-start(bf16[12,64,512]{2,1,0:T(8,128)(2,1)S(1)} %get-tuple-element.143) | copy-start | bytes 2359300
  641.0 15.5 %copy-start.10 = (bf16[512,768]{0,1:T(8,128)(2,1)S(1)}, bf16[512,768]{0,1:T(8,128)(2,1)}, u32[]{:S(2)}) copy-start(bf16[512,768]{0,1:T(8,128)(2,1)} %copy.93) | copy-start | bytes 2359300
  656.5 9.1 copy-start.2
  668.1 12.7 copy-start.18
  787.3 17.7 %copy-start.85 = (f32[1023,512,1]{1,0,2:T(8,128)S(1)}, f32[1023,512,1]{1,0,2:T(8,128)}, u32[]{:S(2)}) copy-start(f32[1023,512,1]{1,0,2:T(8,128)} %constant.145) | copy-start | bytes 6285316
  954.0 17.7 %copy-start.84 = (f32[1023,512,1]{1,0,2:T(8,128)S(1)}, f32[1023,512,1]{1,0,2:T(8,128)}, u32[]{:S(2)}) copy-start(f32[1023,512,1]{1,0,2:T(8,128)} %constant.146) | copy-start | bytes 6285316
  971.7 44.3 %copy-start.9 = (bf16[512,768]{0,1:T(8,128)(2,1)S(1)}, bf16[512,768]{0,1:T(8,128)(2,1)}, u32[]{:S(2)}) copy-start(bf16[512,768]{0,1:T(8,128)(2,1)} %copy-done.8) | copy-start | bytes 2359300
  1071.7 42.0 %copy-start.26 = (bf16[12,64,512]{2,1,0:T(8,128)(2,1)S(1)}, bf16[12,64,512]{2,1,0:T(8,128)(2,1)}, u32[]{:S(2)}) copy-start(bf16[12,64,512]{2,1,0:T(8,128)(2,1)} %get-tuple-element.135) | copy-start | bytes 2359300
  1071.7 42.0 %copy-start.36 = (bf16[768,768]{1,0:T(8,128)(2,1)S(1)}, bf16[768,768]{1,0:T(8,128)(2,1)}, u32[]{:S(2)}) copy-start(bf16[768,768]{1,0:T(8,128)(2,1)} %param.29) | copy-start | bytes 3538948
  1074.3 40.2 %copy-start.28 = (bf16[12,64,512]{2,1,0:T(8,128)(2,1)S(1)}, bf16[12,64,512]{2,1,0:T(8,128)(2,1)}, u32[]{:S(2)}) copy-start(bf16[12,64,512]{2,1,0:T(8,128)(2,1)} %copy-done.27) | copy-start | bytes 2359300
  (74 other events, 211.5 us)
Sparse Core Ops, SparseCore 0:
  429.4 29.8 all-gather.2
  483.7 43.3 reduce-scatter.2
  535.9 27.2 all-gather.4
  580.1 43.3 reduce-scatter.4
  627.6 117.1 all-reduce.13
  1031.3 223.2 all-reduce.11
where the time goes:
time: 1280 us; the launch traced here: 1270 us
  local copies, waits for them, and re-layouts  624 us (49%)
  waiting for transfers between devices  268 us (21%)
  matrix products  253 us (20%)
  blocking collectives  73.5 us (6%)
  other arithmetic  39.7 us (3%)
  between operations  15.8 us (1%)
    unnamed x197, local copies, waits for them, and re-layouts  226 us
    reshape x4, local copies, waits for them, and re-layouts, skewed(): return piece.reshape(head_count, row_count, line_count)[:, :, :row_count]  173 us
    psum x1, waiting for transfers between devices, per_device(): lax.psum((grad_w_query, grad_b_query, grad_w_key, grad_b_key, grad_w_valu...  135 us
    slice x2, local copies, waits for them, and re-layouts, skewed(): piece = flat[:, row_count - 1:row_count - 1 + row_count * line_count]  51 us
    dot_general x1, matrix products, per_device(): jnp.einsum('hjs,sm->hjm', d_key_line, onehot_backward, precision=MAXIMAL_...  44.3 us
    dot_general x1, matrix products, per_device(): jnp.einsum('his,sm->him', d_query_line, onehot_forward, precision=MAXIMAL...  44.2 us
    reduce_scatter x1, waiting for transfers between devices, per_device(): lax.psum_scatter(product(active_low, w_outer), 'mp', scatter_dimension=0,...  42.8 us
    psum x1, blocking collectives, per_device(): lax.psum((grad_w_query, grad_b_query, grad_w_key, grad_b_key, grad_w_valu...  39.1 us
  transfers between devices with their start and end apart: 6, of which 5 were waited for; matrix products, arithmetic and copies ran while one was open for 33% of the time, Pallas kernels for 0%

commit v1 on v0

v1 whole, which is shorter than its diff:
```python
import functools
import math

import jax
import jax.numpy as jnp
import numpy as np
from jax import lax
from jax.experimental import pallas as pl
from jax.experimental.pallas import tpu as pltpu
from jax.sharding import PartitionSpec as P

HEADS = 12
EPS = 1e-06
LOG2E = 1.4426950408889634
TILE = 128
CHUNK = 384
BOTH = ("dp", "mp")
f32 = jnp.float32
bf16 = jnp.bfloat16


def bucket_line(half_rows):
    table_rows = 2 * half_rows
    middle = half_rows // 2
    relative = table_rows - 1 - np.arange(2 * table_rows - 1)
    signed = np.sign(relative)
    absolute = np.where((relative < middle) & (relative > -middle), middle - 1, np.abs(relative))
    log_place = (
        np.ceil(np.log(absolute / middle) / np.log((table_rows - 1) / middle) * (middle - 1))
        + middle
    )
    placed = np.where(absolute <= middle, relative, log_place * signed)
    return (placed + half_rows).astype(np.int32)


def valid_pairs(group_kind, lengths, block_rows):
    capacity = jnp.right_shift(jnp.int32(block_rows), group_kind)
    places = jnp.arange(block_rows, dtype=jnp.int32)
    owner_slot = places // capacity
    offset = places - owner_slot * capacity
    slot_ids = jnp.arange(4, dtype=jnp.int32)
    limits = jnp.sum(
        jnp.where(owner_slot[:, None] == slot_ids[None, :], lengths[None, :], 0), axis=1
    )
    return (owner_slot[:, None] == owner_slot[None, :]) & (offset < limits)[None, :]


def dot(a, b):
    return jnp.dot(a, b, preferred_element_type=f32)


def dot_nt(a, b):
    return lax.dot_general(a, b, (((1,), (1,)), ((), ())), preferred_element_type=f32)


def dot_tn(a, b):
    return lax.dot_general(a, b, (((0,), (0,)), ((), ())), preferred_element_type=f32)


def wide(v):
    return v.astype(f32)


def ln_parts(v):
    average = jnp.mean(v, axis=-1, keepdims=True)
    center = v - average
    root = lax.rsqrt(jnp.mean(center * center, axis=-1, keepdims=True) + EPS)
    return center * root, root


def ln_back(dy, normed, root, gain):
    return (
        ln_back_rows(dy, normed, root, gain),
        jnp.sum(dy * normed, axis=0, keepdims=True),
        jnp.sum(dy, axis=0, keepdims=True),
    )


def ln_back_rows(dy, normed, root, gain):
    dn = dy * gain
    first = jnp.mean(dn, axis=-1, keepdims=True)
    second = jnp.mean(dn * normed, axis=-1, keepdims=True)
    return root * (dn - first - normed * second)


def gelu_parts(v):
    bell = jnp.exp(-0.5 * v * v)
    t = 1.0 / (1.0 + (0.3275911 * math.sqrt(0.5)) * jnp.abs(v))
    poly = t * (
        0.254829592
        + t * (-0.284496736 + t * (1.421413741 + t * (-1.453152027 + t * 1.061405429)))
    )
    tail = 0.5 * poly * bell
    below = jnp.where(v >= 0, 1.0 - tail, tail)
    return v * below, below + v * bell * (1.0 / math.sqrt(2.0 * math.pi))


def skewed(x, keep):
    turned = [
        pltpu.roll(x[:, TILE * b : TILE * (b + 1)], 1, 1, stride=1, stride_axis=0)
        for b in range(5)
    ]
    return [jnp.where(keep, turned[b], turned[b + 1]) for b in range(4)]


def unskewed(tiles, keep):
    zero = jnp.zeros((TILE, TILE), f32)
    turned = [zero] + [pltpu.roll(t, 0, 1, stride=1, stride_axis=0) for t in tiles] + [zero]
    return [jnp.where(keep, turned[b + 1], turned[b]) for b in range(5)]


def attend_kernel(
    q_ref, k_ref, v_ref, key_line_ref, query_line_ref, bias_ref, out_ref, exp_ref, inv_ref, side_ref
):
    lane = lax.broadcasted_iota(jnp.int32, (1, TILE), 1)
    keep = lax.broadcasted_iota(jnp.int32, (TILE, TILE), 1) <= lax.broadcasted_iota(
        jnp.int32, (TILE, TILE), 0
    )
    mine = [lane < 64, lane >= 64]
    scale = LOG2E / math.sqrt(192)
    for h in range(2):
        for t in range(4):
            km = jnp.where(mine[h], k_ref[TILE * t : TILE * (t + 1), :], 0)
            start = 384 - TILE * t
            sk = skewed(dot_nt(km, query_line_ref[start : start + 640, :]), keep)
            for b in range(4):
                side_ref[h, TILE * b : TILE * (b + 1), TILE * t : TILE * (t + 1)] = sk[b].T
        for t in range(4):
            rows = slice(TILE * t, TILE * (t + 1))
            qm = jnp.where(mine[h], q_ref[rows, :], 0)
            start = 384 - TILE * t
            near = skewed(dot_nt(qm, key_line_ref[start : start + 640, :]), keep)
            content = dot_nt(qm, k_ref[...])
            parts = []
            for b in range(4):
                cols = slice(TILE * b, TILE * (b + 1))
                total = content[:, cols] + near[b] + side_ref[h, rows, cols]
                parts.append(total * scale + bias_ref[rows, cols])
            top = jnp.max(
                jnp.maximum(jnp.maximum(parts[0], parts[1]), jnp.maximum(parts[2], parts[3])),
                axis=1,
                keepdims=True,
            )
            low = [jnp.exp2(p - top).astype(bf16) for p in parts]
            total = jnp.sum(
                (wide(low[0]) + wide(low[1])) + (wide(low[2]) + wide(low[3])),
                axis=1,
                keepdims=True,
            )
            exps = jnp.concatenate(low, axis=1)
            exp_ref[h, rows, :] = exps
            inverse = 1.0 / total
            out = (dot(exps, v_ref[...]) * inverse).astype(bf16)
            inverse = jnp.broadcast_to(inverse, (TILE, TILE))
            if h == 0:
                inv_ref[0, rows, :] = inverse
                out_ref[rows, :] = out
            else:
                inv_ref[0, rows, :] = jnp.where(mine[0], inv_ref[0, rows, :], inverse)
                out_ref[rows, :] = jnp.where(mine[0], out_ref[rows, :], out)


def attend(q, k, v, key_line, query_line, bias):
    rows, width = q.shape
    pairs = width // TILE
    col = pl.BlockSpec((rows, TILE), lambda g: (0, g))
    line = pl.BlockSpec((2 * rows, TILE), lambda g: (0, g))
    return pl.pallas_call(
        attend_kernel,
        grid=(pairs,),
        in_specs=[col, col, col, line, line, pl.BlockSpec((rows, rows), lambda g: (0, 0))],
        out_specs=[
            col,
            pl.BlockSpec((2, rows, rows), lambda g: (g, 0, 0)),
            pl.BlockSpec((1, rows, TILE), lambda g: (g, 0, 0)),
        ],
        out_shape=[
            jax.ShapeDtypeStruct((rows, width), bf16),
            jax.ShapeDtypeStruct((2 * pairs, rows, rows), bf16),
            jax.ShapeDtypeStruct((pairs, rows, TILE), f32),
        ],
        scratch_shapes=[pltpu.VMEM((2, rows, rows), f32)],
        compiler_params=pltpu.CompilerParams(vmem_limit_bytes=32 * 1024 * 1024),
        cost_estimate=pl.CostEstimate(
            flops=18_000_000_000, bytes_accessed=16_000_000, transcendentals=3_200_000
        ),
        name="attend",
    )(q, k, v, key_line, query_line, bias)


def attend_back_kernel(
    q_ref,
    k_ref,
    v_ref,
    do_ref,
    exp_ref,
    inv_ref,
    key_line_ref,
    query_line_ref,
    places_ref,
    dq_ref,
    dk_ref,
    dv_ref,
    ds_ref,
    dst_ref,
    query_band,
    key_band,
):
    @pl.when(pl.program_id(0) == 0)
    def _():
        query_band[...] = jnp.zeros_like(query_band)
        key_band[...] = jnp.zeros_like(key_band)

    scale = 1.0 / math.sqrt(192)
    lane = lax.broadcasted_iota(jnp.int32, (1, TILE), 1)
    sub = lax.broadcasted_iota(jnp.int32, (TILE, 1), 0)
    keep = lax.broadcasted_iota(jnp.int32, (TILE, TILE), 1) >= lax.broadcasted_iota(
        jnp.int32, (TILE, TILE), 0
    )
    mine = [lane < 64, lane >= 64]
    mine_t = [sub < 64, sub >= 64]
    flip = (
        lax.broadcasted_iota(jnp.int32, (256, 256), 0)
        + lax.broadcasted_iota(jnp.int32, (256, 256), 1)
        == 255
    )
    flip = flip.astype(f32).astype(bf16)

    def reverse(x):
        return jnp.concatenate([dot(flip, x[256:]), dot(flip, x[:256])], axis=0).astype(bf16)

    q = q_ref[...]
    k = reverse(k_ref[...])
    v = reverse(v_ref[...])
    q_t = q.T
    k_t = k.T
    do = (wide(do_ref[...]) * inv_ref[0]).astype(bf16)
    do_t = do.T
    dv_t = None
    dqs, dks, key_lines, query_lines = [], [], [], []
    for h in range(2):
        dom = jnp.where(mine[h], do, 0)
        for t in range(4):
            rows = slice(TILE * t, TILE * (t + 1))
            dp = dot_nt(dom[rows], v)
            e = jnp.concatenate(
                [dot(exp_ref[h, rows, 256:], flip), dot(exp_ref[h, rows, :256], flip)], axis=1
            )
            ep = e * dp
            mean = jnp.sum(ep, axis=1, keepdims=True) * inv_ref[0, rows, 64 * h : 64 * h + 1]
            ds = ep - e * mean
            ds_ref[h, rows, :] = ds.astype(bf16)
            out = unskewed([ds[:, TILE * b : TILE * (b + 1)] for b in range(4)], keep)
            for b in range(5):
                query_band[h, rows, TILE * (t + b) : TILE * (t + b + 1)] = out[b].astype(bf16)
        for t in range(4):
            rows = slice(TILE * t, TILE * (t + 1))
            turned = [ds_ref[h, TILE * b : TILE * (b + 1), rows].T for b in range(4)]
            for b in range(4):
                dst_ref[h, rows, TILE * b : TILE * (b + 1)] = turned[b]
            out = unskewed([wide(x) for x in turned], keep)
            for b in range(5):
                key_band[h, rows, TILE * (t + b) : TILE * (t + b + 1)] = out[b].astype(bf16)
        part = dot(jnp.where(mine_t[h], do_t, 0), exp_ref[h])
        dv_t = part if dv_t is None else dv_t + part
        dq, dk, key_line, query_line = [], [], [], []
        for i in range(2):
            rows = slice(256 * i, 256 * (i + 1))
            band = slice(256 * i, 256 * i + 768)
            dq.append(dot(ds_ref[h, rows, :], k) + dot(query_band[h, rows, band], key_line_ref[band, :]))
            dk.append(dot(dst_ref[h, rows, :], q) + dot(key_band[h, rows, band], query_line_ref[band, :]))
            key_line.append(dot(jnp.where(mine_t[h], q_t[:, rows], 0), query_band[h, rows, band]))
            query_line.append(dot(jnp.where(mine_t[h], k_t[:, rows], 0), key_band[h, rows, band]))
        dqs.append(jnp.concatenate(dq, axis=0))
        dks.append(jnp.concatenate(dk, axis=0))
        key_lines.append(key_line)
        query_lines.append(query_line)
    size = q.shape[0]
    dq_ref[:size, :] = (jnp.where(mine[0], dqs[0], dqs[1]) * scale).astype(bf16)
    dk_ref[:size, :] = reverse((jnp.where(mine[0], dks[0], dks[1]) * scale).astype(bf16))
    dv_ref[...] = dv_t.T.astype(bf16)
    for lines, ref in ((key_lines, dk_ref), (query_lines, dq_ref)):
        first = lines[0][0] + lines[1][0]
        second = lines[0][1] + lines[1][1]
        whole = jnp.concatenate(
            [first[:, :256], first[:, 256:] + second[:, :512], second[:, 512:]], axis=1
        )
        ref[size:, :] = dot((whole * scale).astype(bf16), places_ref[...]).T.astype(bf16)


def attend_back(q, k, v, do, exps, inverse, key_line, query_line, places, first, count):
    rows = q.shape[0]
    col = pl.BlockSpec((rows, TILE), lambda g: (0, first + g))
    line = pl.BlockSpec((2 * rows, TILE), lambda g: (0, first + g))
    both = pl.BlockSpec((2 * rows, TILE), lambda g: (0, g))
    return pl.pallas_call(
        attend_back_kernel,
        grid=(count,),
        in_specs=[
            col,
            col,
            col,
            col,
            pl.BlockSpec((2, rows, rows), lambda g: (first + g, 0, 0)),
            pl.BlockSpec((1, rows, TILE), lambda g: (first + g, 0, 0)),
            line,
            line,
            pl.BlockSpec((2 * rows, rows), lambda g: (0, 0)),
        ],
        out_specs=[both, both, pl.BlockSpec((rows, TILE), lambda g: (0, g))],
        out_shape=[
            jax.ShapeDtypeStruct((2 * rows, count * TILE), bf16),
            jax.ShapeDtypeStruct((2 * rows, count * TILE), bf16),
            jax.ShapeDtypeStruct((rows, count * TILE), bf16),
        ],
        scratch_shapes=[
            pltpu.VMEM((2, rows, rows), bf16),
            pltpu.VMEM((2, rows, rows), bf16),
            pltpu.VMEM((2, rows, 2 * rows), bf16),
            pltpu.VMEM((2, rows, 2 * rows), bf16),
        ],
        compiler_params=pltpu.CompilerParams(vmem_limit_bytes=40 * 1024 * 1024),
        cost_estimate=pl.CostEstimate(
            flops=count * 4_000_000_000, bytes_accessed=count * 3_000_000, transcendentals=0
        ),
        name="attend_back",
    )(q, k, v, do, exps, inverse, key_line, query_line, places)


def ffn_step(h_ref, w_in, b_in, w_out, slope_ref, active_ref, total_ref):
    for r in range(0, h_ref.shape[0], 256):
        rows = slice(r, r + 256)
        active, slope = gelu_parts(dot(h_ref[rows, :], w_in) + wide(b_in))
        active = active.astype(bf16)
        slope_ref[0, rows, :] = slope.astype(bf16)
        if active_ref is not None:
            active_ref[rows, :] = active
        total_ref[rows, :] += dot(active, w_out)


def ffn_own_kernel(h_ref, win_ref, bin_ref, wout_ref, part_ref, active_ref, slope_ref):
    @pl.when(pl.program_id(0) == 0)
    def _():
        part_ref[...] = jnp.zeros_like(part_ref)

    ffn_step(h_ref, win_ref[0], bin_ref[0, 0], wout_ref[0], slope_ref, active_ref, part_ref)


def ffn_own(h, w_in, b_in, w_out):
    rows, width = h.shape
    units = w_in.shape[-1]
    return pl.pallas_call(
        ffn_own_kernel,
        grid=(units // CHUNK,),
        in_specs=[
            pl.BlockSpec((rows, width), lambda c: (0, 0)),
            pl.BlockSpec((1, width, CHUNK), lambda c: (0, 0, c)),
            pl.BlockSpec((1, 1, CHUNK), lambda c: (0, 0, c)),
            pl.BlockSpec((1, CHUNK, width), lambda c: (0, c, 0)),
        ],
        out_specs=[
            pl.BlockSpec((rows, width), lambda c: (0, 0)),
            pl.BlockSpec((rows, CHUNK), lambda c: (0, c)),
            pl.BlockSpec((1, rows, CHUNK), lambda c: (0, 0, c)),
        ],
        out_shape=[
            jax.ShapeDtypeStruct((rows, width), f32),
            jax.ShapeDtypeStruct((rows, units), bf16),
            jax.ShapeDtypeStruct((1, rows, units), bf16),
        ],
        compiler_params=pltpu.CompilerParams(vmem_limit_bytes=32 * 1024 * 1024),
        cost_estimate=pl.CostEstimate(
            flops=4 * rows * width * units, bytes_accessed=10_000_000, transcendentals=2 * rows * units
        ),
        name="ffn_own",
    )(h, w_in, b_in, w_out)


def ffn_rest_kernel(
    h_ref,
    win_ref,
    bin_ref,
    wout_ref,
    part_ref,
    normed_ref,
    cot_ref,
    vec_ref,
    slope_ref,
    out_ref,
    dpre_ref,
    dbranch_ref,
    sums_ref,
    total_ref,
):
    s, c = pl.program_id(0), pl.program_id(1)

    @pl.when((s == 0) & (c == 0))
    def _():
        total_ref[...] = part_ref[...]

    ffn_step(h_ref, win_ref[0], bin_ref[0, 0], wout_ref[0], slope_ref, None, total_ref)

    @pl.when((s == pl.num_programs(0) - 1) & (c == pl.num_programs(1) - 1))
    def _():
        gain1, shift1, b_outer, gain2, shift2 = [vec_ref[i : i + 1, :] for i in range(5)]
        sums = [jnp.zeros(gain1.shape, f32) for _ in range(3)]
        for r in range(0, h_ref.shape[0], TILE):
            rows = slice(r, r + TILE)
            normed, root = ln_parts(
                normed_ref[rows, :] * gain1 + shift1 + total_ref[rows, :] + b_outer
            )
            out_ref[rows, :] = normed * gain2 + shift2
            dy = wide(cot_ref[rows, :])
            d = ln_back_rows(dy, normed, root, gain2)
            dpre_ref[rows, :] = d
            low = d.astype(bf16)
            dbranch_ref[rows, :] = low
            sums[0] += jnp.sum(dy * normed, axis=0, keepdims=True)
            sums[1] += jnp.sum(dy, axis=0, keepdims=True)
            sums[2] += jnp.sum(wide(low), axis=0, keepdims=True)
        pad = jnp.zeros((5, gain1.shape[1]), f32)
        sums_ref[...] = jnp.concatenate(sums + [pad], axis=0)


def ffn_rest(h, w_in, b_in, w_out, part, normed, cot, vec):
    rows, width = h.shape
    n, _, units = w_in.shape
    full = pl.BlockSpec((rows, width), lambda s, c: (0, 0))
    eight = pl.BlockSpec((8, width), lambda s, c: (0, 0))
    return pl.pallas_call(
        ffn_rest_kernel,
        grid=(n, units // CHUNK),
        in_specs=[
            full,
            pl.BlockSpec((1, width, CHUNK), lambda s, c: (s, 0, c)),
            pl.BlockSpec((1, 1, CHUNK), lambda s, c: (s, 0, c)),
            pl.BlockSpec((1, CHUNK, width), lambda s, c: (s, c, 0)),
            full,
            full,
            full,
            eight,
        ],
        out_specs=[
            pl.BlockSpec((1, rows, CHUNK), lambda s, c: (s, 0, c)),
            full,
            full,
            full,
            eight,
        ],
        out_shape=[
            jax.ShapeDtypeStruct((n, rows, units), bf16),
            jax.ShapeDtypeStruct((rows, width), f32),
            jax.ShapeDtypeStruct((rows, width), f32),
            jax.ShapeDtypeStruct((rows, width), bf16),
            jax.ShapeDtypeStruct((8, width), f32),
        ],
        scratch_shapes=[pltpu.VMEM((rows, width), f32)],
        compiler_params=pltpu.CompilerParams(vmem_limit_bytes=40 * 1024 * 1024),
        cost_estimate=pl.CostEstimate(
            flops=4 * n * rows * width * units,
            bytes_accessed=16_000_000,
            transcendentals=2 * n * rows * units,
        ),
        name="ffn_rest",
    )(h, w_in, b_in, w_out, part, normed, cot, vec)


def ffn_back_kernel(
    db_ref,
    win_ref,
    wout_ref,
    slope_ref,
    win_far_ref,
    wout_far_ref,
    slope_far_ref,
    dpre_ref,
    normed_ref,
    root_ref,
    w_output_ref,
    vec_ref,
    dinner_ref,
    dres_ref,
    dattn_ref,
    dmixed_ref,
    sums_ref,
    total_ref,
    *,
    own,
):
    c = pl.program_id(0)

    @pl.when(c == 0)
    def _():
        total_ref[...] = dpre_ref[...]

    def step(win, wout, slope, out):
        for r in range(0, db_ref.shape[0], 256):
            rows = slice(r, r + 256)
            d = (dot_nt(db_ref[rows, :], wout[0]) * wide(slope[0, rows, :])).astype(bf16)
            if out is not None:
                out[rows, :] = d
            total_ref[rows, :] += dot_nt(d, win[0])

    @pl.when(c < own)
    def _():
        step(win_ref, wout_ref, slope_ref, dinner_ref)

    @pl.when(c >= own)
    def _():
        step(win_far_ref, wout_far_ref, slope_far_ref, None)

    @pl.when(c == pl.num_programs(0) - 1)
    def _():
        gain = vec_ref[0:1, :]
        sums = [jnp.zeros(gain.shape, f32) for _ in range(3)]
        for r in range(0, db_ref.shape[0], TILE):
            rows = slice(r, r + TILE)
            dy = total_ref[rows, :]
            normed = normed_ref[rows, :]
            d = ln_back_rows(dy, normed, root_ref[rows, 0:1], gain)
            dres_ref[rows, :] = d
            low = d.astype(bf16)
            dattn_ref[rows, :] = low
            dmixed_ref[rows, :] = dot_nt(low, w_output_ref[...]).astype(bf16)
            sums[0] += jnp.sum(dy * normed, axis=0, keepdims=True)
            sums[1] += jnp.sum(dy, axis=0, keepdims=True)
            sums[2] += jnp.sum(wide(low), axis=0, keepdims=True)
        pad = jnp.zeros((5, gain.shape[1]), f32)
        sums_ref[...] = jnp.concatenate(sums + [pad], axis=0)


def ffn_back(db, w_in, w_out, slope, far_in, far_out, far_slope, dpre, normed, root, w_output, vec):
    rows, width = db.shape
    units = w_in.shape[-1]
    n = far_in.shape[0]
    own = units // CHUNK
    full = pl.BlockSpec((rows, width), lambda c: (0, 0))
    eight = pl.BlockSpec((8, width), lambda c: (0, 0))

    def near(c):
        return jnp.minimum(c, own - 1)

    def share(c):
        return jnp.maximum(c - own, 0) // own

    def far(c):
        return jnp.maximum(c - own, 0) % own

    return pl.pallas_call(
        functools.partial(ffn_back_kernel, own=own),
        grid=((n + 1) * own,),
        in_specs=[
            full,
            pl.BlockSpec((1, width, CHUNK), lambda c: (0, 0, near(c))),
            pl.BlockSpec((1, CHUNK, width), lambda c: (0, near(c), 0)),
            pl.BlockSpec((1, rows, CHUNK), lambda c: (0, 0, near(c))),
            pl.BlockSpec((1, width, CHUNK), lambda c: (share(c), 0, far(c))),
            pl.BlockSpec((1, CHUNK, width), lambda c: (share(c), far(c), 0)),
            pl.BlockSpec((1, rows, CHUNK), lambda c: (share(c), 0, far(c))),
            full,
            full,
            pl.BlockSpec((rows, TILE), lambda c: (0, 0)),
            pl.BlockSpec((width, width), lambda c: (0, 0)),
            eight,
        ],
        out_specs=[pl.BlockSpec((rows, CHUNK), lambda c: (0, near(c))), full, full, full, eight],
        out_shape=[
            jax.ShapeDtypeStruct((rows, units), bf16),
            jax.ShapeDtypeStruct((rows, width), f32),
            jax.ShapeDtypeStruct((rows, width), bf16),
            jax.ShapeDtypeStruct((rows, width), bf16),
            jax.ShapeDtypeStruct((8, width), f32),
        ],
        scratch_shapes=[pltpu.VMEM((rows, width), f32)],
        compiler_params=pltpu.CompilerParams(vmem_limit_bytes=40 * 1024 * 1024),
        cost_estimate=pl.CostEstimate(
            flops=4 * (n + 1) * rows * width * units, bytes_accessed=20_000_000, transcendentals=0
        ),
        name="ffn_back",
    )(db, w_in, w_out, slope, far_in, far_out, far_slope, dpre, normed, root, w_output, vec)


def ffn_grads_kernel(
    h_ref,
    db_ref,
    active_ref,
    dinner_ref,
    far_h_ref,
    far_db_ref,
    win_ref,
    bin_ref,
    wout_ref,
    out_ref,
    h_t,
    far_t,
    *,
    chunks,
):
    c = pl.program_id(0)
    tail = 4 * CHUNK * chunks

    @pl.when(c == 0)
    def _():
        h_t[...] = h_ref[...].T
        far_t[...] = far_h_ref[...].T
        out_ref[tail:, :] = jnp.zeros_like(out_ref[tail:, :])

    w_in, w_out = win_ref[0], wout_ref[0]
    active, dinner = [], []
    for r in range(0, far_h_ref.shape[0], 256):
        rows = slice(r, r + 256)
        a, slope = gelu_parts(dot(far_h_ref[rows, :], w_in) + wide(bin_ref[0, 0]))
        active.append(a.astype(bf16))
        dinner.append((dot_nt(far_db_ref[rows, :], w_out) * slope).astype(bf16))
    active = jnp.concatenate(active, axis=0)
    dinner = jnp.concatenate(dinner, axis=0)
    base = pl.multiple_of(c * 4 * CHUNK, 4 * CHUNK)
    out_ref[pl.ds(base, 2 * CHUNK), :] = (
        dot(h_t[...], dinner_ref[...]) + dot(far_t[...], dinner)
    ).astype(bf16)
    grad = (dot(active_ref[...].T, db_ref[...]) + dot(active.T, far_db_ref[...])).astype(bf16)
    out_ref[pl.ds(base + 2 * CHUNK, CHUNK), :] = grad[:, :CHUNK]
    out_ref[pl.ds(base + 3 * CHUNK, CHUNK), :] = grad[:, CHUNK:]
    bias = jnp.sum(wide(dinner_ref[...]), axis=0, keepdims=True)
    bias = bias + jnp.sum(wide(dinner), axis=0, keepdims=True)
    place = lax.broadcasted_iota(jnp.int32, (16, 1), 0) == c
    out_ref[tail : tail + 16, :] = jnp.where(place, bias.astype(bf16), out_ref[tail : tail + 16, :])


def ffn_grads(h, db, active, dinner, far_h, far_db, w_in, b_in, w_out, extra):
    rows, width = h.shape
    units = w_in.shape[-1]
    chunks = units // CHUNK
    far = far_h.shape[0]

    def fixed(r, w):
        return pl.BlockSpec((r, w), lambda c: (0, 0))

    total = chunks * 4 * CHUNK + extra
    return pl.pallas_call(
        functools.partial(ffn_grads_kernel, chunks=chunks),
        grid=(chunks,),
        in_specs=[
            fixed(rows, width),
            fixed(rows, width),
            pl.BlockSpec((rows, CHUNK), lambda c: (0, c)),
            pl.BlockSpec((rows, CHUNK), lambda c: (0, c)),
            fixed(far, width),
            fixed(far, width),
            pl.BlockSpec((1, width, CHUNK), lambda c: (0, 0, c)),
            pl.BlockSpec((1, 1, CHUNK), lambda c: (0, 0, c)),
            pl.BlockSpec((1, CHUNK, width), lambda c: (0, c, 0)),
        ],
        out_specs=fixed(total, CHUNK),
        out_shape=jax.ShapeDtypeStruct((total, CHUNK), bf16),
        scratch_shapes=[pltpu.VMEM((width, rows), bf16), pltpu.VMEM((width, far), bf16)],
        compiler_params=pltpu.CompilerParams(vmem_limit_bytes=48 * 1024 * 1024),
        cost_estimate=pl.CostEstimate(
            flops=4 * (rows + 2 * far) * width * units,
            bytes_accessed=16_000_000,
            transcendentals=2 * far * units,
        ),
        name="ffn_grads",
    )(h, db, active, dinner, far_h, far_db, w_in, b_in, w_out)


class Moves:
    def __init__(self, n_dp, n_mp):
        self.n_dp, self.n_mp = n_dp, n_mp
        self.dp = lax.axis_index("dp")
        self.mp = lax.axis_index("mp")
        self.core = self.dp % 2
        self.dp_bits = [("dp", 1 << b) for b in range(1, n_dp.bit_length() - 1)]
        self.mp_bits = [("mp", 1 << b) for b in range(n_mp.bit_length() - 1)]

    def swap(self, x, pair):
        perm = []
        for d in range(self.n_dp):
            for m in range(self.n_mp):
                axis, bit = pair[d % 2]
                dest = (d ^ bit, m) if axis == "dp" else (d, m ^ bit)
                perm.append((d * self.n_mp + m, dest[0] * self.n_mp + dest[1]))
        return lax.ppermute(x, BOTH, perm)

    def side(self, pair):
        values = [((self.dp if axis == "dp" else self.mp) // bit) % 2 for axis, bit in pair]
        return jnp.where(self.core == 0, values[0], values[1])

    def scatter(self, x, pair):
        half = x.shape[0] // 2
        side = self.side(pair)
        sent = lax.dynamic_slice_in_dim(x, (1 - side) * half, half, 0)
        kept = lax.dynamic_slice_in_dim(x, side * half, half, 0)
        return (wide(kept) + wide(self.swap(sent, pair))).astype(bf16)

    def gather(self, x, pair):
        other = self.swap(x, pair)
        side = self.side(pair)
        first = jnp.where(side == 0, x, other)
        second = jnp.where(side == 0, other, x)
        return jnp.concatenate([first, second], axis=0)

    def steps(self, first, second):
        core = ("dp", 1)
        pairs = [(core, core)] + list(zip(first, second, strict=True))
        down = [functools.partial(self.scatter, pair=pair) for pair in pairs]
        up = [functools.partial(self.gather, pair=pair) for pair in reversed(pairs)]
        return down + up


def tie(*arrays):
    return lax.optimization_barrier(arrays)


def per_device(
    inputs,
    cotangent,
    w_query,
    b_query,
    w_key,
    b_key,
    w_value,
    b_value,
    w_output,
    b_output,
    norm1_gain,
    norm1_shift,
    w_inner,
    b_inner,
    w_outer,
    b_outer,
    norm2_gain,
    norm2_shift,
    rel_table,
    rel_gain,
    rel_shift,
    block_group,
    seq_lengths,
    *,
    n_dp,
    n_mp,
):
    rows, width = inputs.shape
    units = w_inner.shape[1]
    moves = Moves(n_dp, n_mp)
    core = ("dp", 1)

    def all_shares(x):
        half = x.shape[0] // 2
        x = lax.dynamic_slice_in_dim(x, moves.core * half, half, 0)[None]
        shares = [x]
        for bit in moves.mp_bits:
            shares = [jnp.concatenate(shares, axis=0)]
            shares.append(moves.swap(shares[0], (bit, bit)))
        got = jnp.concatenate(shares, axis=0)[1:]
        other = moves.swap(got, (core, core))
        first = jnp.where(moves.core == 0, got, other)
        second = jnp.where(moves.core == 0, other, got)
        return jnp.concatenate([first, second], axis=1)

    bias_rows = -(-units // width)
    bias_block = jnp.pad(b_inner, (0, 32 * width - units)).reshape(32, width)
    far_in = all_shares(w_inner)
    far_out = all_shares(jnp.concatenate([w_outer, bias_block], axis=0))
    far_bias = far_out[:, units : units + bias_rows].reshape(n_mp - 1, 1, -1)[:, :, :units]

    line = bucket_line(rows // 2)
    place_ids = np.arange(rows)[None, :]
    forward = jnp.asarray(np.append(line, -1)[:, None] == place_ids).astype(bf16)
    backward = jnp.asarray(np.append(line[::-1], -1)[:, None] == place_ids).astype(bf16)
    rel_normed, rel_root = ln_parts(wide(rel_table))
    rel = (rel_normed * wide(rel_gain) + wide(rel_shift)).astype(bf16)

    def project(left, weight, bias):
        return (dot(left, weight) + wide(bias)).astype(bf16)

    query = project(inputs, w_query, b_query)
    key = project(inputs, w_key, b_key)
    value = project(inputs, w_value, b_value)
    pos_query = project(rel, w_query, b_query)
    pos_key = project(rel, w_key, b_key)
    key_line = dot(forward, pos_key).astype(bf16)
    key_line_back = dot(backward, pos_key).astype(bf16)
    query_line = dot(backward, pos_query).astype(bf16)
    bias = jnp.where(valid_pairs(block_group[0], seq_lengths[0], rows), 0.0, -1e30).astype(f32)

    mixed, exps, inverse = attend(query, key, value, key_line, query_line, bias)

    residual = dot(mixed, w_output) + wide(b_output) + wide(inputs)
    normed1, root1 = ln_parts(residual)
    hidden_low = (normed1 * wide(norm1_gain) + wide(norm1_shift)).astype(bf16)
    root1 = jnp.broadcast_to(root1, (rows, TILE))

    def far(x):
        whole = x
        for bit in moves.mp_bits:
            whole = jnp.concatenate([whole, moves.swap(whole, (bit, bit))], axis=0)
        return whole[rows:]

    far_hidden = far(hidden_low)
    own_in, own_out, own_bias = w_inner[None], w_outer[None], b_inner[None, None]
    part, active, slope = ffn_own(hidden_low, own_in, own_bias, own_out)
    zero = jnp.zeros((width,), bf16)
    vec = jnp.stack(
        [norm1_gain, norm1_shift, b_outer, norm2_gain, norm2_shift, zero, zero, zero]
    ).astype(f32)
    far_slope, layer_out, d_pre2, d_branch, sums2 = ffn_rest(
        hidden_low, far_in, far_bias, far_out, part, normed1, cotangent, vec
    )
    far_branch = far(d_branch)
    d_inner, d_residual, d_attn, d_mixed, sums1 = ffn_back(
        d_branch,
        own_in,
        own_out,
        slope,
        far_in,
        far_out,
        far_slope,
        d_pre2,
        normed1,
        root1,
        w_output,
        vec,
    )
    grad_w_output = dot_tn(mixed, d_attn).astype(bf16)
    ffn = ffn_grads(
        hidden_low,
        d_branch,
        active,
        d_inner,
        far_hidden,
        far_branch,
        own_in,
        own_bias,
        own_out,
        8 * n_dp,
    )

    dp_bits, mp_bits = moves.dp_bits, moves.mp_bits
    turned_bits = dp_bits[1:2] + dp_bits[:1] + dp_bits[2:]
    ffn_steps = moves.steps(dp_bits, turned_bits)
    first = mp_bits + dp_bits
    second = dp_bits[1:2] + mp_bits + dp_bits[:1] + dp_bits[2:]

    both = jnp.concatenate([inputs, rel], axis=0)
    cut = 2 * TILE
    groups = width // cut
    pieces, blocks = [], []
    early = None
    for g in range(groups):
        ffn, d_mixed = tie(ffn, d_mixed)
        if g == groups - 1:
            early = jnp.concatenate(
                [grad_w_output[:, cut * i : cut * (i + 1)] for i in range(groups)] + blocks, axis=0
            )
            blocks = []
            early, d_mixed = tie(early, d_mixed)
        ffn = ffn_steps.pop(0)(ffn)
        d_query, d_key, d_value = attend_back(
            query, key, value, d_mixed, exps, inverse, key_line_back, query_line, backward, 2 * g, 2
        )
        pieces.append((d_query, d_key, d_value))
        blocks.append(dot_tn(both, d_query).astype(bf16))
        blocks.append(dot_tn(both, d_key).astype(bf16))
        blocks.append(dot_tn(inputs, d_value).astype(bf16))
    early_steps = moves.steps(first, second)
    for step in early_steps:
        early = step(early)
    for step in ffn_steps:
        ffn = step(ffn)

    d_query, d_key, d_value = [jnp.concatenate(p, axis=1) for p in zip(*pieces, strict=True)]

    def column_sums(x):
        return jnp.sum(wide(x), axis=0, keepdims=True)

    back = dot_nt(d_query, w_query) + dot_nt(d_key, w_key)
    input_grad = d_residual + back[:rows] + dot_nt(d_value, w_value)
    grad_rel_table, grad_rel_gain, grad_rel_shift = ln_back(
        back[rows:], rel_normed, rel_root, wide(rel_gain)
    )
    vectors = jnp.concatenate(
        [
            sums1,
            sums2,
            column_sums(d_query),
            column_sums(d_key),
            column_sums(d_value),
            grad_rel_gain,
            grad_rel_shift,
            jnp.zeros((11, width), f32),
        ],
        axis=0,
    ).astype(bf16)
    grad_rel_table = grad_rel_table.astype(bf16)
    late = jnp.concatenate(
        blocks
        + [grad_rel_table[:, cut * i : cut * (i + 1)] for i in range(groups)]
        + [vectors[:, cut * i : cut * (i + 1)] for i in range(groups)]
        + [jnp.zeros((256 - 32 * groups, cut), bf16)],
        axis=0,
    )
    for step in moves.steps(first, second):
        late = step(late)

    early, late, ffn = wide(early), wide(late), wide(ffn)

    def rows_of(x, index, size=width):
        return x[index : index + size]

    def columns(parts):
        return jnp.concatenate(parts, axis=1)

    after = 3 * width
    table = columns([rows_of(late, after + rows * i, rows) for i in range(groups)])
    after = after + groups * rows
    vectors = columns([rows_of(late, after + 32 * i, 32) for i in range(groups)])
    grads = []
    for i in range(3):
        parts = [rows_of(early, (groups + 3 * g + i) * width) for g in range(groups - 1)]
        grads.append(columns(parts + [rows_of(late, i * width)]))
    chunks = units // CHUNK
    ffn_in = columns([rows_of(ffn, 4 * CHUNK * c) for c in range(chunks)])
    ffn_out = jnp.concatenate(
        [
            columns([rows_of(ffn, 4 * CHUNK * c + (2 + i) * CHUNK, CHUNK) for i in range(2)])
            for c in range(chunks)
        ],
        axis=0,
    )
    ffn_bias = rows_of(ffn, 4 * CHUNK * chunks, chunks).reshape(units)
    return (
        layer_out,
        input_grad,
        grads[0],
        vectors[16],
        grads[1],
        vectors[17],
        grads[2],
        vectors[18],
        columns([rows_of(early, i * width) for i in range(groups)]),
        vectors[2],
        vectors[0],
        vectors[1],
        ffn_in,
        ffn_bias,
        ffn_out,
        vectors[10],
        vectors[8],
        vectors[9],
        table,
        vectors[19],
        vectors[20],
    )


def solution(mesh):
    n_dp, n_mp = mesh.shape["dp"], mesh.shape["mp"]

    def body(*args):
        return per_device(*args, n_dp=n_dp, n_mp=n_mp)

    split = P(("dp", "mp"), None)
    weights = [P()] * 10 + [P(None, "mp"), P("mp"), P("mp", None)] + [P()] * 6
    return jax.shard_map(
        body,
        mesh=mesh,
        in_specs=(split, split, *weights, P(("dp", "mp")), split),
        out_specs=(
            split,
            split,
            *([P()] * 10),
            P(None, "mp"),
            P("mp"),
            P("mp", None),
            *([P()] * 6),
        ),
        check_vma=False,
    )
```

time: 1280 us -> 420 us (0.33)
  local copies, waits for them, and re-layouts: 624 us -> 59.6 us
  matrix products: 253 us -> 34 us
  waiting for transfers between devices: 268 us -> 102 us
  Pallas kernels: 0 us -> 117 us
  blocking collectives: 73.5 us -> 0 us
  starting transfers between devices: 0.83 us -> 29.6 us
  other arithmetic: 39.7 us -> 67.1 us
    reshape x8 -> x3, local copies, waits for them, and re-layouts: 216 us -> 2.79 us  [the longest x1 1.48 us: per_device(): bias_block = jnp.pad(b_inner, (0, 32 * width - units)).reshape(32, width)]
    dot_general x37 -> x21, matrix products: 237 us -> 34 us  [the longest x8 15.6 us: dot(): return jnp.dot(a, b, preferred_element_type=f32)]
    unnamed x197 -> x198, local copies, waits for them, and re-layouts: 226 us -> 31.5 us
    psum x2 -> x0, waiting for transfers between devices: 135 us -> none  [the longest x1 135 us: per_device(): lax.psum((grad_w_query, grad_b_query, grad_w_key, grad_b_key, grad_w_valu...]
    pallas_call x0 -> x8, Pallas kernels: none -> 117 us  [the longest x3 37.7 us: attend_back(): pl.pallas_call(attend_back_kernel, grid=(count,), in_specs=[col, col, col...]
    ppermute x0 -> x34, waiting for transfers between devices: none -> 102 us  [swap(): return lax.ppermute(x, BOTH, perm)]
    pad x6 -> x1, local copies, waits for them, and re-layouts: 89.2 us -> 0.63 us  [per_device(): bias_block = jnp.pad(b_inner, (0, 32 * width - units)).reshape(32, width)]
    reduce_scatter x2 -> x0, waiting for transfers between devices: 75.1 us -> none  [the longest x1 42.8 us: per_device(): lax.psum_scatter(product(active_low, w_outer), 'mp', scatter_dimension=0,...]
  transfers between devices with their start and end apart: 6 -> 34, of which waited for: 5 -> 15; matrix products, arithmetic and copies ran while one was open for 33% -> 22% of each run, Pallas kernels for 0% -> 21%
where the time goes in v1:
time: 420 us; the launch traced here: 413 us
  Pallas kernels  117 us (28%)
  waiting for transfers between devices  102 us (24%)
  other arithmetic  67.1 us (16%)
  local copies, waits for them, and re-layouts  59.6 us (14%)
  matrix products  34 us (8%)
  starting transfers between devices  29.6 us (7%)
    ppermute x34, waiting for transfers between devices, swap(): return lax.ppermute(x, BOTH, perm)  102 us
    pallas_call x3, Pallas kernels, attend_back(): pl.pallas_call(attend_back_kernel, grid=(count,), in_specs=[col, col, col...  37.7 us
    unnamed x198, local copies, waits for them, and re-layouts  31.5 us
    ppermute x34, starting transfers between devices, swap(): return lax.ppermute(x, BOTH, perm)  29.6 us
    pallas_call x1, Pallas kernels, attend(): pl.pallas_call(attend_kernel, grid=(pairs,), in_specs=[col, col, col, lin...  28.5 us
    pallas_call x1, Pallas kernels, ffn_grads(): pl.pallas_call(functools.partial(ffn_grads_kernel, chunks=chunks), grid=(...  16.9 us
    dot_general x8, matrix products, dot(): return jnp.dot(a, b, preferred_element_type=f32)  15.6 us
    pallas_call x1, Pallas kernels, ffn_back(): pl.pallas_call(functools.partial(ffn_back_kernel, own=own), grid=((n + 1)...  14.4 us
  transfers between devices with their start and end apart: 34, of which 15 were waited for; matrix products, arithmetic and copies ran while one was open for 22% of the time, Pallas kernels for 21%

profile of v1, /device:TPU:0, one launch (start us, length us, event | category | flops | bytes accessed | tf_op | source)
XLA Modules:
  0.0 413.1 jit_solution(5966819160371667540)
XLA Ops:
  16.2 4.1 %fusion.16.query_line_ref = bf16[1024,768]{1,0:T(8,128)(2,1)} fusion(pred[1024,512]{1,0:T(32,128)(4,1)} %constant.364.clone, bf16[512,768]{1,0:T(8,128)(2,1)} %copy-done.63, bf16[768,768]{1,0:T(8,128)(2,1)S(1)} %copy-done, f32[768]{0:T(1024)S(1)} %convert_element_type.265), kind=kOutput, calls=%fused_computation.58 | convolution fusion | flops 1410859008 | bytes 4066304 | tf_op jit(solution)/shard_map/dot_general | solution.py:49
  26.2 28.5 %attend.1 = (bf16[512,768]{1,0:T(8,128)(2,1)S(1)}, bf16[12,512,512]{2,1,0:T(8,128)(2,1)S(1)}, f32[6,512,128]{2,1,0:T(8,128)S(1)}) custom-call(bf16[512,768]{1,0:T(8,128)(2,1)S(1)} %copy-done.32, bf16[512,768]{1,0:T(8,128)(2,1)S(1)} %copy-done.30, bf16[512,768]{1,0:T(8,128)(2,1)S(1)} %add_convert_fusion.8.v_ref, bf16[1024,768]{1,0:T(8,128)(2,1)S(1)} %fusion.15.key_line_ref, ...), custom_call_target="tpu_custom_call" | custom-call | flops 17999998976 | bytes 16000000 | tf_op jit(solution)/shard_map/attend/pallas_call | solution.py:168
  73.5 8.3 %ffn_own.1 = (f32[512,768]{1,0:T(8,128)S(1)}, bf16[512,1536]{1,0:T(8,128)(2,1)S(1)}, bf16[1,512,1536]{2,1,0:T(8,128)(2,1)S(1)}) custom-call(bf16[512,768]{1,0:T(8,128)(2,1)} %get-tuple-element.102.h_ref, bf16[1,768,1536]{2,1,0:T(8,128)(2,1)S(1)} %bitcast.68, bf16[1,1,1536]{2,1,0:T(2,128)(2,1)S(1)} %broadcast_in_dim.98.bin_ref, bf16[1,1536,768]{2,1,0:T(8,128)(2,1)S(1)} %bitcast.65), custom_call_target="tpu_custom_call" | custom-call | flops 2415919104 | bytes 10000000 | tf_op jit(solution)/shard_map/ffn_own/pallas_call | solution.py:352
  94.3 11.3 %ffn_rest.1 = (bf16[1,512,1536]{2,1,0:T(8,128)(2,1)S(1)}, f32[512,768]{1,0:T(8,128)}, f32[512,768]{1,0:T(8,128)S(1)}, bf16[512,768]{1,0:T(8,128)(2,1)}, f32[8,768]{1,0:T(8,128)S(1)}) custom-call(bf16[512,768]{1,0:T(8,128)(2,1)} %get-tuple-element.102.h_ref, bf16[1,768,1536]{2,1,0:T(8,128)(2,1)S(1)} %pad_maximum_fusion.3.win_ref.win_far_ref, ...), custom_call_target="tpu_custom_call" | custom-call | flops 2415919104 | bytes 16000000 | tf_op jit(solution)/shard_map/ffn_rest/pallas_call | solution.py:430
  116.4 14.4 %ffn_back.1 = (bf16[512,1536]{1,0:T(8,128)(2,1)S(1)}, f32[512,768]{1,0:T(8,128)S(1)}, bf16[512,768]{1,0:T(8,128)(2,1)S(1)}, bf16[512,768]{1,0:T(8,128)(2,1)S(1)}, f32[8,768]{1,0:T(8,128)S(1)}) custom-call(bf16[512,768]{1,0:T(8,128)(2,1)} %get-tuple-element.57.db_ref, bf16[1,768,1536]{2,1,0:T(8,128)(2,1)} %bitcast.66, bf16[1,1536,768]{2,1,0:T(8,128)(2,1)} %bitcast.63, ...), custom_call_target="tpu_custom_call" | custom-call | flops 4831838208 | bytes 20000000 | tf_op jit(solution)/shard_map/ffn_back/pallas_call | solution.py:549
  134.6 16.9 %ffn_grads.1 = bf16[6272,384]{1,0:T(8,128)(2,1)} custom-call(bf16[512,768]{1,0:T(8,128)(2,1)} %get-tuple-element.102.h_ref, bf16[512,768]{1,0:T(8,128)(2,1)} %get-tuple-element.57.db_ref, bf16[512,1536]{1,0:T(8,128)(2,1)S(1)} %copy-done.37, bf16[512,1536]{1,0:T(8,128)(2,1)} %copy-done.25, bf16[512,768]{1,0:T(8,128)(2,1)} %collective-permute-done.4.far_h_ref, ...), custom_call_target="tpu_custom_call" | custom-call | flops 7247757312 | bytes 16000000 | tf_op jit(solution)/shard_map/ffn_grads/pallas_call | solution.py:640
  155.3 12.7 %attend_back.3 = (bf16[1024,256]{1,0:T(8,128)(2,1)S(1)}, bf16[1024,256]{1,0:T(8,128)(2,1)S(1)}, bf16[512,256]{1,0:T(8,128)(2,1)S(1)}) custom-call(bf16[512,768]{1,0:T(8,128)(2,1)S(1)} %copy-done.33, bf16[512,768]{1,0:T(8,128)(2,1)S(1)} %copy-done.31, bf16[512,768]{1,0:T(8,128)(2,1)S(1)} %copy-done.35, bf16[512,768]{1,0:T(8,128)(2,1)S(1)} %get-tuple-element.79.do_ref, ...), custom_call_target="tpu_custom_call" | custom-call | flops 8000000000 | bytes 6000000 | tf_op jit(solution)/shard_map/attend_back/pallas_call | solution.py:296
  175.9 12.5 %attend_back.4 = (bf16[1024,256]{1,0:T(8,128)(2,1)S(1)}, bf16[1024,256]{1,0:T(8,128)(2,1)S(1)}, bf16[512,256]{1,0:T(8,128)(2,1)S(1)}) custom-call(bf16[512,768]{1,0:T(8,128)(2,1)S(1)} %copy-done.33, bf16[512,768]{1,0:T(8,128)(2,1)S(1)} %copy-done.31, bf16[512,768]{1,0:T(8,128)(2,1)S(1)} %copy-done.35, bf16[512,768]{1,0:T(8,128)(2,1)S(1)} %get-tuple-element.79.do_ref, ...), custom_call_target="tpu_custom_call" | custom-call | flops 8000000000 | bytes 6000000 | tf_op jit(solution)/shard_map/attend_back/pallas_call | solution.py:296
  194.4 12.5 %attend_back.5 = (bf16[1024,256]{1,0:T(8,128)(2,1)S(1)}, bf16[1024,256]{1,0:T(8,128)(2,1)S(1)}, bf16[512,256]{1,0:T(8,128)(2,1)S(1)}) custom-call(bf16[512,768]{1,0:T(8,128)(2,1)S(1)} %copy-done.33, bf16[512,768]{1,0:T(8,128)(2,1)S(1)} %copy-done.31, bf16[512,768]{1,0:T(8,128)(2,1)S(1)} %copy-done.35, bf16[512,768]{1,0:T(8,128)(2,1)S(1)} %get-tuple-element.79.do_ref, ...), custom_call_target="tpu_custom_call" | custom-call | flops 8000000000 | bytes 6000000 | tf_op jit(solution)/shard_map/attend_back/pallas_call | solution.py:296
  219.0 3.7 convolution_add_fusion
  239.7 5.7 %collective-permute-done.28 = bf16[784,384]{1,0:T(8,128)(2,1)} collective-permute-done((bf16[784,384]{1,0:T(8,128)(2,1)S(1)}, bf16[784,384]{1,0:T(8,128)(2,1)}, u32[]{:S(2)}, u32[]{:S(2)}) %collective-permute-start.28) | collective-permute-done | bytes 602144 | tf_op jit(solution)/shard_map/ppermute | solution.py:683
  253.2 10.6 %collective-permute-done.29 = bf16[392,384]{1,0:T(8,128)(2,1)S(1)} collective-permute-done((bf16[392,384]{1,0:T(8,128)(2,1)}, bf16[392,384]{1,0:T(8,128)(2,1)S(1)}, u32[]{:S(2)}, u32[]{:S(2)}) %collective-permute-start.29) | collective-permute-done | bytes 301088 | tf_op jit(solution)/shard_map/ppermute | solution.py:683
  264.8 14.4 %collective-permute-done.30 = bf16[392,384]{1,0:T(8,128)(2,1)S(1)} collective-permute-done((bf16[392,384]{1,0:T(8,128)(2,1)S(1)}, bf16[392,384]{1,0:T(8,128)(2,1)S(1)}, u32[]{:S(2)}, u32[]{:S(2)}) %collective-permute-start.30) | collective-permute-done | bytes 301088 | tf_op jit(solution)/shard_map/ppermute | solution.py:683
  283.6 7.2 %collective-permute-done.21 = bf16[256,256]{1,0:T(8,128)(2,1)S(1)} collective-permute-done((bf16[256,256]{1,0:T(8,128)(2,1)S(1)}, bf16[256,256]{1,0:T(8,128)(2,1)S(1)}, u32[]{:S(2)}, u32[]{:S(2)}) %collective-permute-start.21) | collective-permute-done | bytes 131104 | tf_op jit(solution)/shard_map/ppermute | solution.py:683
  292.7 4.0 collective-permute-done.22
  297.2 5.4 %collective-permute-done.23 = bf16[128,256]{1,0:T(8,128)(2,1)S(1)} collective-permute-done((bf16[128,256]{1,0:T(8,128)(2,1)S(1)}, bf16[128,256]{1,0:T(8,128)(2,1)S(1)}, u32[]{:S(2)}, u32[]{:S(2)}) %collective-permute-start.23) | collective-permute-done | bytes 65568 | tf_op jit(solution)/shard_map/ppermute | solution.py:683
  310.9 15.2 %collective-permute-done.25 = bf16[512,256]{1,0:T(8,128)(2,1)} collective-permute-done((bf16[512,256]{1,0:T(8,128)(2,1)S(1)}, bf16[512,256]{1,0:T(8,128)(2,1)}, u32[]{:S(2)}, u32[]{:S(2)}) %collective-permute-start.25) | collective-permute-done | bytes 262176 | tf_op jit(solution)/shard_map/ppermute | solution.py:683
  340.0 5.0 %collective-permute-done.12 = bf16[216,256]{1,0:T(8,128)(2,1)S(1)} collective-permute-done((bf16[216,256]{1,0:T(8,128)(2,1)S(1)}, bf16[216,256]{1,0:T(8,128)(2,1)S(1)}, u32[]{:S(2)}, u32[]{:S(2)}) %collective-permute-start.12) | collective-permute-done | bytes 110624 | tf_op jit(solution)/shard_map/ppermute | solution.py:683
  345.8 5.9 %collective-permute-done.13 = bf16[216,256]{1,0:T(8,128)(2,1)S(1)} collective-permute-done((bf16[216,256]{1,0:T(8,128)(2,1)S(1)}, bf16[216,256]{1,0:T(8,128)(2,1)S(1)}, u32[]{:S(2)}, u32[]{:S(2)}) %collective-permute-start.13) | collective-permute-done | bytes 110624 | tf_op jit(solution)/shard_map/ppermute | solution.py:683
  352.2 5.6 %collective-permute-done.14 = bf16[432,256]{1,0:T(8,128)(2,1)S(1)} collective-permute-done((bf16[432,256]{1,0:T(8,128)(2,1)S(1)}, bf16[432,256]{1,0:T(8,128)(2,1)S(1)}, u32[]{:S(2)}, u32[]{:S(2)}) %collective-permute-start.14) | collective-permute-done | bytes 221216 | tf_op jit(solution)/shard_map/ppermute | solution.py:683
  360.3 5.9 %collective-permute-done.15 = bf16[864,256]{1,0:T(8,128)(2,1)S(1)} collective-permute-done((bf16[864,256]{1,0:T(8,128)(2,1)S(1)}, bf16[864,256]{1,0:T(8,128)(2,1)S(1)}, u32[]{:S(2)}, u32[]{:S(2)}) %collective-permute-start.15) | collective-permute-done | bytes 442400 | tf_op jit(solution)/shard_map/ppermute | solution.py:683
  371.1 8.5 %collective-permute-done.16 = bf16[1728,256]{1,0:T(8,128)(2,1)S(1)} collective-permute-done((bf16[1728,256]{1,0:T(8,128)(2,1)S(1)}, bf16[1728,256]{1,0:T(8,128)(2,1)S(1)}, u32[]{:S(2)}, u32[]{:S(2)}) %collective-permute-start.16) | collective-permute-done | bytes 884768 | tf_op jit(solution)/shard_map/ppermute | solution.py:683
  382.4 4.8 %maximum_convert_fusion = f32[6272,384]{1,0:T(8,128)} fusion(bf16[3136,384]{1,0:T(8,128)(2,1)S(1)} %get-tuple-element.126, bf16[3136,384]{1,0:T(8,128)(2,1)S(1)} %get-tuple-element.125), kind=kLoop, calls=%fused_computation | loop fusion | flops 9633792 | bytes 14450688 | tf_op jit(solution)/shard_map/convert_element_type | solution.py:61
  395.5 6.8 %maximum_maximum_fusion = f32[1536,768]{1,0:T(8,128)} fusion(f32[384,384]{1,0:T(8,128)S(1)} %get-tuple-element.118, f32[384,384]{1,0:T(8,128)S(1)} %get-tuple-element.119, f32[384,384]{1,0:T(8,128)S(1)} %get-tuple-element.120, f32[384,384]{1,0:T(8,128)S(1)} %get-tuple-element.121, f32[384,384]{1,0:T(8,128)S(1)} %get-tuple-element.122, ...), kind=kLoop, calls=%fused_computation.3 | loop fusion | flops 8257536 | bytes 9437184 | tf_op jit(solution)/shard_map/concatenate | solution.py:924
  (407 shorter events, 179.5 us)
Async XLA Ops:
  3.2 55.5 %collective-permute-start = (bf16[1,384,1536]{2,1,0:T(8,128)(2,1)}, bf16[1,384,1536]{2,1,0:T(8,128)(2,1)}, u32[]{:S(2)}, u32[]{:S(2)}) collective-permute-start(bf16[1,384,1536]{2,1,0:T(8,128)(2,1)} %dynamic-slice_bitcast_fusion), channel_id=1, source_target_pairs={{0,1},{1,0},{2,3},{3,2},{4,5},{5,4},{6,7},{7,6},{8,9},{9,8},{10,11... | collective-permute-start | bytes 3538952 | tf_op jit(solution)/shard_map/ppermute | solution.py:683
  10.0 49.5 %collective-permute-start.2 = (bf16[1,784,768]{2,1,0:T(8,128)(2,1)}, bf16[1,784,768]{2,1,0:T(8,128)(2,1)}, u32[]{:S(2)}, u32[]{:S(2)}) collective-permute-start(bf16[1,784,768]{2,1,0:T(8,128)(2,1)} %fusion.25), channel_id=1, source_target_pairs={{0,1},{1,0},{2,3},{3,2},{4,5},{5,4},{6,7},{7,6},{8,9},{9,8},{10,11... | collective-permute-start | bytes 3612680 | tf_op jit(solution)/shard_map/ppermute | solution.py:683
  58.7 23.1 %collective-permute-start.1 = (bf16[1,384,1536]{2,1,0:T(8,128)(2,1)}, bf16[1,384,1536]{2,1,0:T(8,128)(2,1)}, u32[]{:S(2)}, u32[]{:S(2)}) collective-permute-start(bf16[1,384,1536]{2,1,0:T(8,128)(2,1)} %collective-permute-done), channel_id=1, source_target_pairs={{0,2},{1,3},{2,0},{3,1},{4,6},{5,7},{6,4},{7,5},{8,10},{9,11},{10,... | collective-permute-start | bytes 3538952 | tf_op jit(solution)/shard_map/ppermute | solution.py:683
  59.5 26.0 %collective-permute-start.3 = (bf16[1,784,768]{2,1,0:T(8,128)(2,1)}, bf16[1,784,768]{2,1,0:T(8,128)(2,1)}, u32[]{:S(2)}, u32[]{:S(2)}) collective-permute-start(bf16[1,784,768]{2,1,0:T(8,128)(2,1)} %collective-permute-done.2), channel_id=1, source_target_pairs={{0,2},{1,3},{2,0},{3,1},{4,6},{5,7},{6,4},{7,5},{8,10},{9,11},{10,... | collective-permute-start | bytes 3612680 | tf_op jit(solution)/shard_map/ppermute | solution.py:683
  61.4 73.1 %collective-permute-start.4 = (bf16[512,768]{1,0:T(8,128)(2,1)}, bf16[512,768]{1,0:T(8,128)(2,1)}, u32[]{:S(2)}, u32[]{:S(2)}) collective-permute-start(bf16[512,768]{1,0:T(8,128)(2,1)} %get-tuple-element.102.h_ref), channel_id=1, source_target_pairs={{0,1},{1,0},{2,3},{3,2},{4,5},{5,4},{6,7},{7,6},{8,9},{9,8},{10,11... | collective-permute-start | bytes 2359304 | tf_op jit(solution)/shard_map/ppermute | solution.py:683
  108.5 26.0 %collective-permute-start.5 = (bf16[512,768]{1,0:T(8,128)(2,1)}, bf16[512,768]{1,0:T(8,128)(2,1)}, u32[]{:S(2)}, u32[]{:S(2)}) collective-permute-start(bf16[512,768]{1,0:T(8,128)(2,1)} %get-tuple-element.57.db_ref), channel_id=1, source_target_pairs={{0,1},{1,0},{2,3},{3,2},{4,5},{5,4},{6,7},{7,6},{8,9},{9,8},{10,11... | collective-permute-start | bytes 2359304 | tf_op jit(solution)/shard_map/ppermute | solution.py:683
  153.6 17.7 %collective-permute-start.6 = (bf16[3136,384]{1,0:T(8,128)(2,1)S(1)}, bf16[3136,384]{1,0:T(8,128)(2,1)}, u32[]{:S(2)}, u32[]{:S(2)}) collective-permute-start(bf16[3136,384]{1,0:T(8,128)(2,1)S(1)} %constant_dynamic-slice_fusion.13), channel_id=1, source_target_pairs={{0,2},{1,3},{2,0},{3,1},{4,6},{5,7},{6,4},{7,5},{8,10},{9,11},{10,... | collective-permute-start | bytes 7225352 | tf_op jit(solution)/shard_map/ppermute | solution.py:683
  173.8 17.4 %collective-permute-start.7 = (bf16[1568,384]{1,0:T(8,128)(2,1)S(1)}, bf16[1568,384]{1,0:T(8,128)(2,1)S(1)}, u32[]{:S(2)}, u32[]{:S(2)}) collective-permute-start(bf16[1568,384]{1,0:T(8,128)(2,1)S(1)} %constant_dynamic-slice_fusion.12), channel_id=1, source_target_pairs={{0,4},{1,5},{2,10},{3,11},{4,0},{5,1},{6,14},{7,15},{8,12},{9,13},... | collective-permute-start | bytes 3612680 | tf_op jit(solution)/shard_map/ppermute | solution.py:683
  235.1 14.9 %collective-permute-start.18 = (bf16[2048,256]{1,0:T(8,128)(2,1)S(1)}, bf16[2048,256]{1,0:T(8,128)(2,1)}, u32[]{:S(2)}, u32[]{:S(2)}) collective-permute-start(bf16[2048,256]{1,0:T(8,128)(2,1)S(1)} %constant_dynamic-slice_fusion.6), channel_id=1, source_target_pairs={{0,2},{1,3},{2,0},{3,1},{4,6},{5,7},{6,4},{7,5},{8,10},{9,11},{10,... | collective-permute-start | bytes 3145736 | tf_op jit(solution)/shard_map/ppermute | solution.py:683
  239.7 41.9 %collective-permute-start.8 = (bf16[3456,256]{1,0:T(8,128)(2,1)}, bf16[3456,256]{1,0:T(8,128)(2,1)}, u32[]{:S(2)}, u32[]{:S(2)}) collective-permute-start(bf16[3456,256]{1,0:T(8,128)(2,1)} %constant_dynamic-slice_fusion.11), channel_id=1, source_target_pairs={{0,2},{1,3},{2,0},{3,1},{4,6},{5,7},{6,4},{7,5},{8,10},{9,11},{10,... | collective-permute-start | bytes 5308424 | tf_op jit(solution)/shard_map/ppermute | solution.py:683
  247.5 16.3 %collective-permute-start.29 = (bf16[392,384]{1,0:T(8,128)(2,1)}, bf16[392,384]{1,0:T(8,128)(2,1)S(1)}, u32[]{:S(2)}, u32[]{:S(2)}) collective-permute-start(bf16[392,384]{1,0:T(8,128)(2,1)} %constant_dynamic-slice_fusion), channel_id=1, source_target_pairs={{0,16},{1,17},{2,18},{3,19},{4,20},{5,21},{6,22},{7,23},{8,24},{9,... | collective-permute-start | bytes 903176 | tf_op jit(solution)/shard_map/ppermute | solution.py:683
  251.7 12.3 %collective-permute-start.19 = (bf16[1024,256]{1,0:T(8,128)(2,1)S(1)}, bf16[1024,256]{1,0:T(8,128)(2,1)S(1)}, u32[]{:S(2)}, u32[]{:S(2)}) collective-permute-start(bf16[1024,256]{1,0:T(8,128)(2,1)S(1)} %constant_dynamic-slice_fusion.5), channel_id=1, source_target_pairs={{0,1},{1,0},{2,10},{3,11},{4,5},{5,4},{6,14},{7,15},{8,9},{9,8},{1... | collective-permute-start | bytes 1572872 | tf_op jit(solution)/shard_map/ppermute | solution.py:683
  263.9 15.3 %collective-permute-start.30 = (bf16[392,384]{1,0:T(8,128)(2,1)S(1)}, bf16[392,384]{1,0:T(8,128)(2,1)S(1)}, u32[]{:S(2)}, u32[]{:S(2)}) collective-permute-start(bf16[392,384]{1,0:T(8,128)(2,1)S(1)} %add_convert_fusion.14), channel_id=1, source_target_pairs={{0,16},{1,17},{2,18},{3,19},{4,20},{5,21},{6,22},{7,23},{8,24},{9,... | collective-permute-start | bytes 903176 | tf_op jit(solution)/shard_map/ppermute | solution.py:683
  264.2 15.3 %collective-permute-start.20 = (bf16[512,256]{1,0:T(8,128)(2,1)S(1)}, bf16[512,256]{1,0:T(8,128)(2,1)S(1)}, u32[]{:S(2)}, u32[]{:S(2)}) collective-permute-start(bf16[512,256]{1,0:T(8,128)(2,1)S(1)} %constant_dynamic-slice_fusion.4), channel_id=1, source_target_pairs={{0,4},{1,5},{2,3},{3,2},{4,0},{5,1},{6,7},{7,6},{8,12},{9,13},{10,... | collective-permute-start | bytes 786440 | tf_op jit(solution)/shard_map/ppermute | solution.py:683
  279.3 17.6 %collective-permute-start.31 = (bf16[784,384]{1,0:T(8,128)(2,1)S(1)}, bf16[784,384]{1,0:T(8,128)(2,1)S(1)}, u32[]{:S(2)}, u32[]{:S(2)}) collective-permute-start(bf16[784,384]{1,0:T(8,128)(2,1)S(1)} %pad_maximum_fusion.14), channel_id=1, source_target_pairs={{0,8},{1,9},{2,6},{3,7},{4,12},{5,13},{6,2},{7,3},{8,0},{9,1},{10,... | collective-permute-start | bytes 1806344 | tf_op jit(solution)/shard_map/ppermute | solution.py:683
  291.0 17.3 %collective-permute-start.9 = (bf16[1728,256]{1,0:T(8,128)(2,1)S(1)}, bf16[1728,256]{1,0:T(8,128)(2,1)S(1)}, u32[]{:S(2)}, u32[]{:S(2)}) collective-permute-start(bf16[1728,256]{1,0:T(8,128)(2,1)S(1)} %constant_dynamic-slice_fusion.10), channel_id=1, source_target_pairs={{0,1},{1,0},{2,10},{3,11},{4,5},{5,4},{6,14},{7,15},{8,9},{9,8},{1... | collective-permute-start | bytes 2654216 | tf_op jit(solution)/shard_map/ppermute | solution.py:683
  304.2 28.5 %collective-permute-start.32 = (bf16[1568,384]{1,0:T(8,128)(2,1)}, bf16[1568,384]{1,0:T(8,128)(2,1)}, u32[]{:S(2)}, u32[]{:S(2)}) collective-permute-start(bf16[1568,384]{1,0:T(8,128)(2,1)} %pad_maximum_fusion.11), channel_id=1, source_target_pairs={{0,4},{1,5},{2,10},{3,11},{4,0},{5,1},{6,14},{7,15},{8,12},{9,13},... | collective-permute-start | bytes 3612680 | tf_op jit(solution)/shard_map/ppermute | solution.py:683
  307.7 18.4 %collective-permute-start.25 = (bf16[512,256]{1,0:T(8,128)(2,1)S(1)}, bf16[512,256]{1,0:T(8,128)(2,1)}, u32[]{:S(2)}, u32[]{:S(2)}) collective-permute-start(bf16[512,256]{1,0:T(8,128)(2,1)S(1)} %pad_maximum_fusion.17), channel_id=1, source_target_pairs={{0,4},{1,5},{2,3},{3,2},{4,0},{5,1},{6,7},{7,6},{8,12},{9,13},{10,... | collective-permute-start | bytes 786440 | tf_op jit(solution)/shard_map/ppermute | solution.py:683
  309.4 21.3 %collective-permute-start.10 = (bf16[864,256]{1,0:T(8,128)(2,1)}, bf16[864,256]{1,0:T(8,128)(2,1)S(1)}, u32[]{:S(2)}, u32[]{:S(2)}) collective-permute-start(bf16[864,256]{1,0:T(8,128)(2,1)} %constant_dynamic-slice_fusion.9), channel_id=1, source_target_pairs={{0,4},{1,5},{2,3},{3,2},{4,0},{5,1},{6,7},{7,6},{8,12},{9,13},{10,... | collective-permute-start | bytes 1327112 | tf_op jit(solution)/shard_map/ppermute | solution.py:683
  327.2 12.6 %collective-permute-start.26 = (bf16[1024,256]{1,0:T(8,128)(2,1)S(1)}, bf16[1024,256]{1,0:T(8,128)(2,1)S(1)}, u32[]{:S(2)}, u32[]{:S(2)}) collective-permute-start(bf16[1024,256]{1,0:T(8,128)(2,1)S(1)} %pad_maximum_fusion.15), channel_id=1, source_target_pairs={{0,1},{1,0},{2,10},{3,11},{4,5},{5,4},{6,14},{7,15},{8,9},{9,8},{1... | collective-permute-start | bytes 1572872 | tf_op jit(solution)/shard_map/ppermute | solution.py:683
  345.8 12.8 %collective-permute-start.27 = (bf16[2048,256]{1,0:T(8,128)(2,1)S(1)}, bf16[2048,256]{1,0:T(8,128)(2,1)S(1)}, u32[]{:S(2)}, u32[]{:S(2)}) collective-permute-start(bf16[2048,256]{1,0:T(8,128)(2,1)S(1)} %pad_maximum_fusion.12), channel_id=1, source_target_pairs={{0,2},{1,3},{2,0},{3,1},{4,6},{5,7},{6,4},{7,5},{8,10},{9,11},{10,... | collective-permute-start | bytes 3145736 | tf_op jit(solution)/shard_map/ppermute | solution.py:683
  352.1 29.2 %collective-permute-start.33 = (bf16[3136,384]{1,0:T(8,128)(2,1)S(1)}, bf16[3136,384]{1,0:T(8,128)(2,1)S(1)}, u32[]{:S(2)}, u32[]{:S(2)}) collective-permute-start(bf16[3136,384]{1,0:T(8,128)(2,1)S(1)} %pad_maximum_fusion.2), channel_id=1, source_target_pairs={{0,2},{1,3},{2,0},{3,1},{4,6},{5,7},{6,4},{7,5},{8,10},{9,11},{10,... | collective-permute-start | bytes 7225352 | tf_op jit(solution)/shard_map/ppermute | solution.py:683
  366.5 13.1 %collective-permute-start.16 = (bf16[1728,256]{1,0:T(8,128)(2,1)S(1)}, bf16[1728,256]{1,0:T(8,128)(2,1)S(1)}, u32[]{:S(2)}, u32[]{:S(2)}) collective-permute-start(bf16[1728,256]{1,0:T(8,128)(2,1)S(1)} %pad_maximum_fusion.13), channel_id=1, source_target_pairs={{0,1},{1,0},{2,10},{3,11},{4,5},{5,4},{6,14},{7,15},{8,9},{9,8},{1... | collective-permute-start | bytes 2654216 | tf_op jit(solution)/shard_map/ppermute | solution.py:683
  381.3 21.0 %collective-permute-start.17 = (bf16[3456,256]{1,0:T(8,128)(2,1)}, bf16[3456,256]{1,0:T(8,128)(2,1)}, u32[]{:S(2)}, u32[]{:S(2)}) collective-permute-start(bf16[3456,256]{1,0:T(8,128)(2,1)} %pad_maximum_fusion.8), channel_id=1, source_target_pairs={{0,2},{1,3},{2,0},{3,1},{4,6},{5,7},{6,4},{7,5},{8,10},{9,11},{10,... | collective-permute-start | bytes 5308424 | tf_op jit(solution)/shard_map/ppermute | solution.py:683
  (102 other events, 565.2 us)

commit v2 on v1

--- a/solution.py
+++ b/solution.py
@@ -33,18 +33,6 @@
     return (placed + half_rows).astype(np.int32)
 
 
-def valid_pairs(group_kind, lengths, block_rows):
-    capacity = jnp.right_shift(jnp.int32(block_rows), group_kind)
-    places = jnp.arange(block_rows, dtype=jnp.int32)
-    owner_slot = places // capacity
-    offset = places - owner_slot * capacity
-    slot_ids = jnp.arange(4, dtype=jnp.int32)
-    limits = jnp.sum(
-        jnp.where(owner_slot[:, None] == slot_ids[None, :], lengths[None, :], 0), axis=1
-    )
-    return (owner_slot[:, None] == owner_slot[None, :]) & (offset < limits)[None, :]
-
-
 def dot(a, b):
     return jnp.dot(a, b, preferred_element_type=f32)
 
@@ -66,14 +54,6 @@
     center = v - average
     root = lax.rsqrt(jnp.mean(center * center, axis=-1, keepdims=True) + EPS)
     return center * root, root
-
-
-def ln_back(dy, normed, root, gain):
-    return (
-        ln_back_rows(dy, normed, root, gain),
-        jnp.sum(dy * normed, axis=0, keepdims=True),
-        jnp.sum(dy, axis=0, keepdims=True),
-    )
 
 
 def ln_back_rows(dy, normed, root, gain):
@@ -95,6 +75,83 @@
     return v * below, below + v * bell * (1.0 / math.sqrt(2.0 * math.pi))
 
 
+def pre_kernel(
+    x_ref,
+    table_ref,
+    gain_ref,
+    shift_ref,
+    wq_ref,
+    bq_ref,
+    wk_ref,
+    bk_ref,
+    wv_ref,
+    bv_ref,
+    forward_ref,
+    backward_ref,
+    q_ref,
+    k_ref,
+    v_ref,
+    key_line_ref,
+    key_back_ref,
+    query_line_ref,
+    both_t_ref,
+    both_ref,
+):
+    rows = x_ref.shape[0]
+
+    @pl.when(pl.program_id(0) == 0)
+    def _():
+        both_ref[:rows, :] = x_ref[...]
+        normed, _ = ln_parts(wide(table_ref[...]))
+        rel = normed * wide(gain_ref[...])[None, :] + wide(shift_ref[...])[None, :]
+        both_ref[rows:, :] = rel.astype(bf16)
+        both_t_ref[...] = both_ref[...].T
+
+    def project(w_ref, b_ref, part):
+        return (dot(both_ref[part, :], w_ref[...]) + wide(b_ref[...])[None, :]).astype(bf16)
+
+    here, there = slice(0, rows), slice(rows, 2 * rows)
+    q_ref[...] = project(wq_ref, bq_ref, here)
+    k_ref[...] = project(wk_ref, bk_ref, here)
+    v_ref[...] = project(wv_ref, bv_ref, here)
+    pos_query = project(wq_ref, bq_ref, there)
+    pos_key = project(wk_ref, bk_ref, there)
+    key_line_ref[...] = dot(forward_ref[...], pos_key).astype(bf16)
+    key_back_ref[...] = dot(backward_ref[...], pos_key).astype(bf16)
+    query_line_ref[...] = dot(backward_ref[...], pos_query).astype(bf16)
+
+
+def pre(x, table, gain, shift, w_q, b_q, w_k, b_k, w_v, b_v, forward, backward):
+    rows, width = x.shape
+    cut = 2 * TILE
+
+    def fixed(r, w):
+        return pl.BlockSpec((r, w), lambda c: (0, 0))
+
+    whole = pl.BlockSpec((width,), lambda c: (0,))
+    weight = pl.BlockSpec((width, cut), lambda c: (0, c))
+    vector = pl.BlockSpec((cut,), lambda c: (c,))
+    one = pl.BlockSpec((rows, cut), lambda c: (0, c))
+    two = pl.BlockSpec((2 * rows, cut), lambda c: (0, c))
+    return pl.pallas_call(
+        pre_kernel,
+        grid=(width // cut,),
+        in_specs=[fixed(rows, width), fixed(rows, width), whole, whole]
+        + [weight, vector] * 3
+        + [fixed(2 * rows, rows)] * 2,
+        out_specs=[one] * 3 + [two] * 3 + [fixed(width, 2 * rows)],
+        out_shape=[jax.ShapeDtypeStruct((rows, width), bf16)] * 3
+        + [jax.ShapeDtypeStruct((2 * rows, width), bf16)] * 3
+        + [jax.ShapeDtypeStruct((width, 2 * rows), bf16)],
+        scratch_shapes=[pltpu.VMEM((2 * rows, width), bf16)],
+        compiler_params=pltpu.CompilerParams(vmem_limit_bytes=32 * 1024 * 1024),
+        cost_estimate=pl.CostEstimate(
+            flops=5_500_000_000, bytes_accessed=14_000_000, transcendentals=0
+        ),
+        name="pre",
+    )(x, table, gain, shift, w_q, b_q, w_k, b_k, w_v, b_v, forward, backward)
+
+
 def skewed(x, keep):
     turned = [
         pltpu.roll(x[:, TILE * b : TILE * (b + 1)], 1, 1, stride=1, stride_axis=0)
@@ -110,8 +167,33 @@
 
 
 def attend_kernel(
-    q_ref, k_ref, v_ref, key_line_ref, query_line_ref, bias_ref, out_ref, exp_ref, inv_ref, side_ref
+    group_ref,
+    lengths_ref,
+    q_ref,
+    k_ref,
+    v_ref,
+    key_line_ref,
+    query_line_ref,
+    out_ref,
+    exp_ref,
+    inv_ref,
+    side_ref,
+    bias_ref,
 ):
+    @pl.when(pl.program_id(0) == 0)
+    def _():
+        size = bias_ref.shape[0]
+        shift = size.bit_length() - 1 - group_ref[0]
+        row = lax.broadcasted_iota(jnp.int32, (size, 1), 0)
+        col = lax.broadcasted_iota(jnp.int32, (1, size), 1)
+        owner = jnp.right_shift(col, shift)
+        limit = jnp.zeros((1, size), jnp.int32)
+        for slot in range(4):
+            limit = jnp.where(owner == slot, lengths_ref[0, slot], limit)
+        owner = jnp.where(col - jnp.left_shift(owner, shift) < limit, owner, -1)
+        valid = jnp.right_shift(row, shift) == owner
+        bias_ref[...] = jnp.where(valid, 0.0, -1e30).astype(f32)
+
     lane = lax.broadcasted_iota(jnp.int32, (1, TILE), 1)
     keep = lax.broadcasted_iota(jnp.int32, (TILE, TILE), 1) <= lax.broadcasted_iota(
         jnp.int32, (TILE, TILE), 0
@@ -160,15 +242,16 @@
                 out_ref[rows, :] = jnp.where(mine[0], out_ref[rows, :], out)
 
 
-def attend(q, k, v, key_line, query_line, bias):
+def attend(group, lengths, q, k, v, key_line, query_line):
     rows, width = q.shape
     pairs = width // TILE
     col = pl.BlockSpec((rows, TILE), lambda g: (0, g))
     line = pl.BlockSpec((2 * rows, TILE), lambda g: (0, g))
+    scalars = pl.BlockSpec(memory_space=pltpu.SMEM)
     return pl.pallas_call(
         attend_kernel,
         grid=(pairs,),
-        in_specs=[col, col, col, line, line, pl.BlockSpec((rows, rows), lambda g: (0, 0))],
+        in_specs=[scalars, scalars, col, col, col, line, line],
         out_specs=[
             col,
             pl.BlockSpec((2, rows, rows), lambda g: (g, 0, 0)),
@@ -179,13 +262,13 @@
             jax.ShapeDtypeStruct((2 * pairs, rows, rows), bf16),
             jax.ShapeDtypeStruct((pairs, rows, TILE), f32),
         ],
-        scratch_shapes=[pltpu.VMEM((2, rows, rows), f32)],
+        scratch_shapes=[pltpu.VMEM((2, rows, rows), f32), pltpu.VMEM((rows, rows), f32)],
         compiler_params=pltpu.CompilerParams(vmem_limit_bytes=32 * 1024 * 1024),
         cost_estimate=pl.CostEstimate(
             flops=18_000_000_000, bytes_accessed=16_000_000, transcendentals=3_200_000
         ),
         name="attend",
-    )(q, k, v, key_line, query_line, bias)
+    )(group, lengths, q, k, v, key_line, query_line)
 
 
 def attend_back_kernel(
@@ -198,9 +281,11 @@
     key_line_ref,
     query_line_ref,
     places_ref,
+    both_t_ref,
     dq_ref,
     dk_ref,
     dv_ref,
+    grad_ref,
     ds_ref,
     dst_ref,
     query_band,
@@ -286,10 +371,16 @@
             [first[:, :256], first[:, 256:] + second[:, :512], second[:, 512:]], axis=1
         )
         ref[size:, :] = dot((whole * scale).astype(bf16), places_ref[...]).T.astype(bf16)
-
-
-def attend_back(q, k, v, do, exps, inverse, key_line, query_line, places, first, count):
-    rows = q.shape[0]
+    width = both_t_ref.shape[0]
+    grad_ref[0, :width, :] = dot(both_t_ref[...], dq_ref[...]).astype(bf16)
+    grad_ref[0, width : 2 * width, :] = dot(both_t_ref[...], dk_ref[...]).astype(bf16)
+    grad_ref[0, 2 * width :, :] = dot(both_t_ref[:, :size], dv_ref[...]).astype(bf16)
+
+
+def attend_back(
+    q, k, v, do, exps, inverse, key_line, query_line, places, both_t, first, count
+):
+    rows, width = q.shape
     col = pl.BlockSpec((rows, TILE), lambda g: (0, first + g))
     line = pl.BlockSpec((2 * rows, TILE), lambda g: (0, first + g))
     both = pl.BlockSpec((2 * rows, TILE), lambda g: (0, g))
@@ -306,12 +397,19 @@
             line,
             line,
             pl.BlockSpec((2 * rows, rows), lambda g: (0, 0)),
-        ],
-        out_specs=[both, both, pl.BlockSpec((rows, TILE), lambda g: (0, g))],
+            pl.BlockSpec((width, 2 * rows), lambda g: (0, 0)),
+        ],
+        out_specs=[
+            both,
+            both,
+            pl.BlockSpec((rows, TILE), lambda g: (0, g)),
+            pl.BlockSpec((1, 3 * width, TILE), lambda g: (g // 2, 0, g % 2)),
+        ],
         out_shape=[
             jax.ShapeDtypeStruct((2 * rows, count * TILE), bf16),
             jax.ShapeDtypeStruct((2 * rows, count * TILE), bf16),
             jax.ShapeDtypeStruct((rows, count * TILE), bf16),
+            jax.ShapeDtypeStruct((count // 2, 3 * width, 2 * TILE), bf16),
         ],
         scratch_shapes=[
             pltpu.VMEM((2, rows, rows), bf16),
@@ -324,13 +422,13 @@
             flops=count * 4_000_000_000, bytes_accessed=count * 3_000_000, transcendentals=0
         ),
         name="attend_back",
-    )(q, k, v, do, exps, inverse, key_line, query_line, places)
+    )(q, k, v, do, exps, inverse, key_line, query_line, places, both_t)
 
 
 def ffn_step(h_ref, w_in, b_in, w_out, slope_ref, active_ref, total_ref):
     for r in range(0, h_ref.shape[0], 256):
         rows = slice(r, r + 256)
-        active, slope = gelu_parts(dot(h_ref[rows, :], w_in) + wide(b_in))
+        active, slope = gelu_parts(dot(h_ref[rows, :], w_in) + b_in)
         active = active.astype(bf16)
         slope_ref[0, rows, :] = slope.astype(bf16)
         if active_ref is not None:
@@ -338,42 +436,85 @@
         total_ref[rows, :] += dot(active, w_out)
 
 
-def ffn_own_kernel(h_ref, win_ref, bin_ref, wout_ref, part_ref, active_ref, slope_ref):
-    @pl.when(pl.program_id(0) == 0)
-    def _():
+def ffn_own_kernel(
+    mixed_ref,
+    wo_ref,
+    bo_ref,
+    x_ref,
+    gain_ref,
+    shift_ref,
+    win_ref,
+    bin_ref,
+    wout_ref,
+    h_ref,
+    normed_ref,
+    root_ref,
+    part_ref,
+    active_ref,
+    slope_ref,
+    bias_ref,
+):
+    c = pl.program_id(0)
+
+    @pl.when(c == 0)
+    def _():
+        bias_ref[...] = wide(bin_ref[...])[None, :]
+        bias, gain, shift = [wide(r[...])[None, :] for r in (bo_ref, gain_ref, shift_ref)]
+        for r in range(0, x_ref.shape[0], TILE):
+            rows = slice(r, r + TILE)
+            residual = dot(mixed_ref[rows, :], wo_ref[...]) + bias + wide(x_ref[rows, :])
+            normed, root = ln_parts(residual)
+            normed_ref[rows, :] = normed
+            root_ref[rows, :] = jnp.broadcast_to(root, (TILE, TILE))
+            h_ref[rows, :] = (normed * gain + shift).astype(bf16)
         part_ref[...] = jnp.zeros_like(part_ref)
 
-    ffn_step(h_ref, win_ref[0], bin_ref[0, 0], wout_ref[0], slope_ref, active_ref, part_ref)
-
-
-def ffn_own(h, w_in, b_in, w_out):
-    rows, width = h.shape
+    b_in = bias_ref[:, pl.ds(pl.multiple_of(c * CHUNK, TILE), CHUNK)]
+    ffn_step(h_ref, win_ref[...], b_in, wout_ref[...], slope_ref, active_ref, part_ref)
+
+
+def ffn_own(mixed, w_output, b_output, x, gain, shift, w_in, b_in, w_out):
+    rows, width = x.shape
     units = w_in.shape[-1]
+    full = pl.BlockSpec((rows, width), lambda c: (0, 0))
+    vector = pl.BlockSpec((width,), lambda c: (0,))
     return pl.pallas_call(
         ffn_own_kernel,
         grid=(units // CHUNK,),
         in_specs=[
-            pl.BlockSpec((rows, width), lambda c: (0, 0)),
-            pl.BlockSpec((1, width, CHUNK), lambda c: (0, 0, c)),
-            pl.BlockSpec((1, 1, CHUNK), lambda c: (0, 0, c)),
-            pl.BlockSpec((1, CHUNK, width), lambda c: (0, c, 0)),
+            full,
+            pl.BlockSpec((width, width), lambda c: (0, 0)),
+            vector,
+            full,
+            vector,
+            vector,
+            pl.BlockSpec((width, CHUNK), lambda c: (0, c)),
+            pl.BlockSpec((units,), lambda c: (0,)),
+            pl.BlockSpec((CHUNK, width), lambda c: (c, 0)),
         ],
         out_specs=[
-            pl.BlockSpec((rows, width), lambda c: (0, 0)),
+            full,
+            full,
+            pl.BlockSpec((rows, TILE), lambda c: (0, 0)),
+            full,
             pl.BlockSpec((rows, CHUNK), lambda c: (0, c)),
             pl.BlockSpec((1, rows, CHUNK), lambda c: (0, 0, c)),
         ],
         out_shape=[
+            jax.ShapeDtypeStruct((rows, width), bf16),
+            jax.ShapeDtypeStruct((rows, width), f32),
+            jax.ShapeDtypeStruct((rows, TILE), f32),
             jax.ShapeDtypeStruct((rows, width), f32),
             jax.ShapeDtypeStruct((rows, units), bf16),
             jax.ShapeDtypeStruct((1, rows, units), bf16),
         ],
+        scratch_shapes=[pltpu.VMEM((1, units), f32)],
         compiler_params=pltpu.CompilerParams(vmem_limit_bytes=32 * 1024 * 1024),
         cost_estimate=pl.CostEstimate(
-            flops=4 * rows * width * units, bytes_accessed=10_000_000, transcendentals=2 * rows * units
+            flops=4 * rows * width * units, bytes_accessed=14_000_000, transcendentals=2 * rows * units
         ),
         name="ffn_own",
-    )(h, w_in, b_in, w_out)
+    )(mixed, w_output, b_output, x, gain, shift, w_in, b_in, w_out)
 
 
 def ffn_rest_kernel(
@@ -381,28 +522,52 @@
     win_ref,
     bin_ref,
     wout_ref,
+    win2_ref,
+    bin2_ref,
+    wout2_ref,
     part_ref,
     normed_ref,
     cot_ref,
-    vec_ref,
+    gain1_ref,
+    shift1_ref,
+    b_outer_ref,
+    gain2_ref,
+    shift2_ref,
     slope_ref,
     out_ref,
     dpre_ref,
     dbranch_ref,
     sums_ref,
     total_ref,
+    *,
+    steps,
+    chunk,
+    chunks,
 ):
-    s, c = pl.program_id(0), pl.program_id(1)
-
-    @pl.when((s == 0) & (c == 0))
+    c = pl.program_id(0)
+
+    @pl.when(c == 0)
     def _():
         total_ref[...] = part_ref[...]
 
-    ffn_step(h_ref, win_ref[0], bin_ref[0, 0], wout_ref[0], slope_ref, None, total_ref)
-
-    @pl.when((s == pl.num_programs(0) - 1) & (c == pl.num_programs(1) - 1))
-    def _():
-        gain1, shift1, b_outer, gain2, shift2 = [vec_ref[i : i + 1, :] for i in range(5)]
+    def step(win, b_in, wout):
+        start = 0 if chunks == 1 else pl.multiple_of(c % chunks * chunk, TILE)
+        bias = wide(b_in[0, 0:1, pl.ds(start, chunk)])
+        ffn_step(h_ref, win[0], bias, wout[0], slope_ref, None, total_ref)
+
+    @pl.when(c < steps)
+    def _():
+        step(win_ref, bin_ref, wout_ref)
+
+    @pl.when(c >= steps)
+    def _():
+        step(win2_ref, bin2_ref, wout2_ref)
+
+    @pl.when(c == 2 * steps - 1)
+    def _():
+        gain1, shift1, b_outer, gain2, shift2 = [
+            wide(r[...])[None, :] for r in (gain1_ref, shift1_ref, b_outer_ref, gain2_ref, shift2_ref)
+        ]
         sums = [jnp.zeros(gain1.shape, f32) for _ in range(3)]
         for r in range(0, h_ref.shape[0], TILE):
             rows = slice(r, r + TILE)
@@ -422,33 +587,50 @@
         sums_ref[...] = jnp.concatenate(sums + [pad], axis=0)
 
 
-def ffn_rest(h, w_in, b_in, w_out, part, normed, cot, vec):
+def far_specs(n, width, units, chunk, base, steps):
+    chunks = units // chunk
+
+    def place(c):
+        c = jnp.clip(c - base, 0, steps - 1)
+        return c // chunks, c % chunks
+
+    return (
+        pl.BlockSpec((1, width, chunk), lambda c: (place(c)[0], 0, place(c)[1])),
+        pl.BlockSpec((1, 16, width), lambda c: (place(c)[0], units // 16, 0)),
+        pl.BlockSpec((1, chunk, width), lambda c: (place(c)[0], place(c)[1], 0)),
+    )
+
+
+def ffn_rest(h, got, other, part, normed, cot, vectors):
     rows, width = h.shape
-    n, _, units = w_in.shape
-    full = pl.BlockSpec((rows, width), lambda s, c: (0, 0))
-    eight = pl.BlockSpec((8, width), lambda s, c: (0, 0))
+    n, _, units = got[0].shape
+    chunk = min(CHUNK, units)
+    chunks = units // chunk
+    steps = n * chunks
+    full = pl.BlockSpec((rows, width), lambda c: (0, 0))
+    vector = pl.BlockSpec((width,), lambda c: (0,))
+    eight = pl.BlockSpec((8, width), lambda c: (0, 0))
     return pl.pallas_call(
-        ffn_rest_kernel,
-        grid=(n, units // CHUNK),
+        functools.partial(ffn_rest_kernel, steps=steps, chunk=chunk, chunks=chunks),
+        grid=(2 * steps,),
         in_specs=[
             full,
-            pl.BlockSpec((1, width, CHUNK), lambda s, c: (s, 0, c)),
-            pl.BlockSpec((1, 1, CHUNK), lambda s, c: (s, 0, c)),
-            pl.BlockSpec((1, CHUNK, width), lambda s, c: (s, c, 0)),
+            *far_specs(n, width, units, chunk, 0, steps),
+            *far_specs(n, width, units, chunk, steps, steps),
+            full,
+            full,
+            full,
+            *([vector] * 5),
+        ],
+        out_specs=[
+            pl.BlockSpec((1, rows, chunk), lambda c: (c // chunks, 0, c % chunks)),
             full,
             full,
             full,
             eight,
         ],
-        out_specs=[
-            pl.BlockSpec((1, rows, CHUNK), lambda s, c: (s, 0, c)),
-            full,
-            full,
-            full,
-            eight,
-        ],
         out_shape=[
-            jax.ShapeDtypeStruct((n, rows, units), bf16),
+            jax.ShapeDtypeStruct((2 * n, rows, units), bf16),
             jax.ShapeDtypeStruct((rows, width), f32),
             jax.ShapeDtypeStruct((rows, width), f32),
             jax.ShapeDtypeStruct((rows, width), bf16),
@@ -457,12 +639,12 @@
         scratch_shapes=[pltpu.VMEM((rows, width), f32)],
         compiler_params=pltpu.CompilerParams(vmem_limit_bytes=40 * 1024 * 1024),
         cost_estimate=pl.CostEstimate(
-            flops=4 * n * rows * width * units,
+            flops=8 * n * rows * width * units,
             bytes_accessed=16_000_000,
-            transcendentals=2 * n * rows * units,
+            transcendentals=4 * n * rows * units,
         ),
         name="ffn_rest",
-    )(h, w_in, b_in, w_out, part, normed, cot, vec)
+    )(h, got[0], got[1], got[1], other[0], other[1], other[1], part, normed, cot, *vectors)
 
 
 def ffn_back_kernel(
@@ -470,22 +652,27 @@
     win_ref,
     wout_ref,
     slope_ref,
-    win_far_ref,
-    wout_far_ref,
-    slope_far_ref,
+    win1_ref,
+    wout1_ref,
+    win2_ref,
+    wout2_ref,
+    far_slope_ref,
     dpre_ref,
     normed_ref,
     root_ref,
     w_output_ref,
-    vec_ref,
+    mixed_ref,
+    gain_ref,
     dinner_ref,
     dres_ref,
-    dattn_ref,
     dmixed_ref,
+    grad_ref,
     sums_ref,
     total_ref,
+    dattn_ref,
     *,
     own,
+    steps,
 ):
     c = pl.program_id(0)
 
@@ -496,22 +683,26 @@
     def step(win, wout, slope, out):
         for r in range(0, db_ref.shape[0], 256):
             rows = slice(r, r + 256)
-            d = (dot_nt(db_ref[rows, :], wout[0]) * wide(slope[0, rows, :])).astype(bf16)
+            d = (dot_nt(db_ref[rows, :], wout) * wide(slope[0, rows, :])).astype(bf16)
             if out is not None:
                 out[rows, :] = d
-            total_ref[rows, :] += dot_nt(d, win[0])
+            total_ref[rows, :] += dot_nt(d, win)
 
     @pl.when(c < own)
     def _():
-        step(win_ref, wout_ref, slope_ref, dinner_ref)
-
-    @pl.when(c >= own)
-    def _():
-        step(win_far_ref, wout_far_ref, slope_far_ref, None)
+        step(win_ref[...], wout_ref[...], slope_ref, dinner_ref)
+
+    @pl.when((c >= own) & (c < own + steps))
+    def _():
+        step(win1_ref[0], wout1_ref[0], far_slope_ref, None)
+
+    @pl.when(c >= own + steps)
+    def _():
+        step(win2_ref[0], wout2_ref[0], far_slope_ref, None)
 
     @pl.when(c == pl.num_programs(0) - 1)
     def _():
-        gain = vec_ref[0:1, :]
+        gain = wide(gain_ref[...])[None, :]
         sums = [jnp.zeros(gain.shape, f32) for _ in range(3)]
         for r in range(0, db_ref.shape[0], TILE):
             rows = slice(r, r + TILE)
@@ -527,57 +718,90 @@
             sums[2] += jnp.sum(wide(low), axis=0, keepdims=True)
         pad = jnp.zeros((5, gain.shape[1]), f32)
         sums_ref[...] = jnp.concatenate(sums + [pad], axis=0)
-
-
-def ffn_back(db, w_in, w_out, slope, far_in, far_out, far_slope, dpre, normed, root, w_output, vec):
+        width = gain.shape[1]
+        grad = dot(mixed_ref[...].T, dattn_ref[...]).astype(bf16)
+        for i in range(width // 256):
+            grad_ref[width * i : width * (i + 1), :] = grad[:, 256 * i : 256 * (i + 1)]
+
+
+def ffn_back(
+    db, w_in, w_out, slope, got, other, far_slope, dpre, normed, root, w_output, mixed, gain
+):
     rows, width = db.shape
-    units = w_in.shape[-1]
-    n = far_in.shape[0]
-    own = units // CHUNK
+    own_units = w_in.shape[-1]
+    n, _, units = got[0].shape
+    own = own_units // CHUNK
+    chunk = min(CHUNK, units)
+    chunks = units // chunk
+    steps = n * chunks
     full = pl.BlockSpec((rows, width), lambda c: (0, 0))
     eight = pl.BlockSpec((8, width), lambda c: (0, 0))
 
     def near(c):
         return jnp.minimum(c, own - 1)
 
-    def share(c):
-        return jnp.maximum(c - own, 0) // own
-
     def far(c):
-        return jnp.maximum(c - own, 0) % own
-
+        return jnp.maximum(c - own, 0)
+
+    first = far_specs(n, width, units, chunk, own, steps)
+    second = far_specs(n, width, units, chunk, own + steps, steps)
     return pl.pallas_call(
-        functools.partial(ffn_back_kernel, own=own),
-        grid=((n + 1) * own,),
+        functools.partial(ffn_back_kernel, own=own, steps=steps),
+        grid=(own + 2 * steps,),
         in_specs=[
             full,
-            pl.BlockSpec((1, width, CHUNK), lambda c: (0, 0, near(c))),
-            pl.BlockSpec((1, CHUNK, width), lambda c: (0, near(c), 0)),
+            pl.BlockSpec((width, CHUNK), lambda c: (0, near(c))),
+            pl.BlockSpec((CHUNK, width), lambda c: (near(c), 0)),
             pl.BlockSpec((1, rows, CHUNK), lambda c: (0, 0, near(c))),
-            pl.BlockSpec((1, width, CHUNK), lambda c: (share(c), 0, far(c))),
-            pl.BlockSpec((1, CHUNK, width), lambda c: (share(c), far(c), 0)),
-            pl.BlockSpec((1, rows, CHUNK), lambda c: (share(c), 0, far(c))),
+            first[0],
+            first[2],
+            second[0],
+            second[2],
+            pl.BlockSpec((1, rows, chunk), lambda c: (far(c) // chunks, 0, far(c) % chunks)),
             full,
             full,
             pl.BlockSpec((rows, TILE), lambda c: (0, 0)),
             pl.BlockSpec((width, width), lambda c: (0, 0)),
+            full,
+            pl.BlockSpec((width,), lambda c: (0,)),
+        ],
+        out_specs=[
+            pl.BlockSpec((rows, CHUNK), lambda c: (0, near(c))),
+            full,
+            full,
+            pl.BlockSpec((width * width // 256, 256), lambda c: (0, 0)),
             eight,
         ],
-        out_specs=[pl.BlockSpec((rows, CHUNK), lambda c: (0, near(c))), full, full, full, eight],
         out_shape=[
-            jax.ShapeDtypeStruct((rows, units), bf16),
+            jax.ShapeDtypeStruct((rows, own_units), bf16),
             jax.ShapeDtypeStruct((rows, width), f32),
             jax.ShapeDtypeStruct((rows, width), bf16),
-            jax.ShapeDtypeStruct((rows, width), bf16),
+            jax.ShapeDtypeStruct((width * width // 256, 256), bf16),
             jax.ShapeDtypeStruct((8, width), f32),
         ],
-        scratch_shapes=[pltpu.VMEM((rows, width), f32)],
-        compiler_params=pltpu.CompilerParams(vmem_limit_bytes=40 * 1024 * 1024),
+        scratch_shapes=[pltpu.VMEM((rows, width), f32), pltpu.VMEM((rows, width), bf16)],
+        compiler_params=pltpu.CompilerParams(vmem_limit_bytes=44 * 1024 * 1024),
         cost_estimate=pl.CostEstimate(
-            flops=4 * (n + 1) * rows * width * units, bytes_accessed=20_000_000, transcendentals=0
+            flops=16 * rows * width * width, bytes_accessed=22_000_000, transcendentals=0
         ),
         name="ffn_back",
-    )(db, w_in, w_out, slope, far_in, far_out, far_slope, dpre, normed, root, w_output, vec)
+    )(
+        db,
+        w_in,
+        w_out,
+        slope,
+        got[0],
+        got[1],
+        other[0],
+        other[1],
+        far_slope,
+        dpre,
+        normed,
+        root,
+        w_output,
+        mixed,
+        gain,
+    )
 
 
 def ffn_grads_kernel(
@@ -593,6 +817,7 @@
     out_ref,
     h_t,
     far_t,
+    bias_ref,
     *,
     chunks,
 ):
@@ -601,15 +826,17 @@
 
     @pl.when(c == 0)
     def _():
+        bias_ref[...] = wide(bin_ref[...])[None, :]
         h_t[...] = h_ref[...].T
         far_t[...] = far_h_ref[...].T
         out_ref[tail:, :] = jnp.zeros_like(out_ref[tail:, :])
 
-    w_in, w_out = win_ref[0], wout_ref[0]
+    w_in, w_out = win_ref[...], wout_ref[...]
+    b_in = bias_ref[:, pl.ds(pl.multiple_of(c * CHUNK, TILE), CHUNK)]
     active, dinner = [], []
     for r in range(0, far_h_ref.shape[0], 256):
         rows = slice(r, r + 256)
-        a, slope = gelu_parts(dot(far_h_ref[rows, :], w_in) + wide(bin_ref[0, 0]))
+        a, slope = gelu_parts(dot(far_h_ref[rows, :], w_in) + b_in)
         active.append(a.astype(bf16))
         dinner.append((dot_nt(far_db_ref[rows, :], w_out) * slope).astype(bf16))
     active = jnp.concatenate(active, axis=0)
@@ -647,13 +874,17 @@
             pl.BlockSpec((rows, CHUNK), lambda c: (0, c)),
             fixed(far, width),
             fixed(far, width),
-            pl.BlockSpec((1, width, CHUNK), lambda c: (0, 0, c)),
-            pl.BlockSpec((1, 1, CHUNK), lambda c: (0, 0, c)),
-            pl.BlockSpec((1, CHUNK, width), lambda c: (0, c, 0)),
+            pl.BlockSpec((width, CHUNK), lambda c: (0, c)),
+            pl.BlockSpec((units,), lambda c: (0,)),
+            pl.BlockSpec((CHUNK, width), lambda c: (c, 0)),
         ],
         out_specs=fixed(total, CHUNK),
         out_shape=jax.ShapeDtypeStruct((total, CHUNK), bf16),
-        scratch_shapes=[pltpu.VMEM((width, rows), bf16), pltpu.VMEM((width, far), bf16)],
+        scratch_shapes=[
+            pltpu.VMEM((width, rows), bf16),
+            pltpu.VMEM((width, far), bf16),
+            pltpu.VMEM((1, units), f32),
+        ],
         compiler_params=pltpu.CompilerParams(vmem_limit_bytes=48 * 1024 * 1024),
         cost_estimate=pl.CostEstimate(
             flops=4 * (rows + 2 * far) * width * units,
@@ -662,6 +893,75 @@
         ),
         name="ffn_grads",
     )(h, db, active, dinner, far_h, far_db, w_in, b_in, w_out)
+
+
+def late_kernel(
+    dq_ref,
+    dq2_ref,
+    dk_ref,
+    dk2_ref,
+    dv_ref,
+    dv2_ref,
+    wq_ref,
+    wk_ref,
+    table_ref,
+    gain_ref,
+    sums1_ref,
+    sums2_ref,
+    grad_ref,
+    out_ref,
+):
+    rows, width = table_ref.shape
+    split = dq_ref.shape[1]
+    there = slice(rows, 2 * rows)
+    gain = wide(gain_ref[...])[None, :]
+
+    def column_sums(a, b):
+        return jnp.concatenate(
+            [jnp.sum(wide(x[...]), axis=0, keepdims=True) for x in (a, b)], axis=1
+        )
+
+    out_ref[: 3 * width, :] = grad_ref[0]
+    dy = dot_nt(dq_ref[there, :], wq_ref[:, :split]) + dot_nt(dq2_ref[there, :], wq_ref[:, split:])
+    dy = dy + dot_nt(dk_ref[there, :], wk_ref[:, :split])
+    dy = dy + dot_nt(dk2_ref[there, :], wk_ref[:, split:])
+    normed, root = ln_parts(wide(table_ref[...]))
+    table = ln_back_rows(dy, normed, root, gain).astype(bf16)
+    vectors = jnp.concatenate(
+        [
+            sums1_ref[...],
+            sums2_ref[...],
+            column_sums(dq_ref, dq2_ref),
+            column_sums(dk_ref, dk2_ref),
+            column_sums(dv_ref, dv2_ref),
+            jnp.sum(dy * normed, axis=0, keepdims=True),
+            jnp.sum(dy, axis=0, keepdims=True),
+            jnp.zeros((11, width), f32),
+        ],
+        axis=0,
+    ).astype(bf16)
+    base = 3 * width
+    for i in range(width // 256):
+        out_ref[base + rows * i : base + rows * (i + 1), :] = table[:, 256 * i : 256 * (i + 1)]
+    base = base + rows * (width // 256)
+    for i in range(width // 256):
+        out_ref[base + 32 * i : base + 32 * (i + 1), :] = vectors[:, 256 * i : 256 * (i + 1)]
+    base = base + 32 * (width // 256)
+    out_ref[base:, :] = jnp.zeros((out_ref.shape[0] - base, 256), bf16)
+
+
+def late_sums(d_query, d_key, d_value, w_query, w_key, table, gain, sums1, sums2, grad):
+    rows, width = table.shape
+    total = -(-(3 * width + (rows + 32) * (width // 256)) // 256) * 256
+    return pl.pallas_call(
+        late_kernel,
+        out_shape=jax.ShapeDtypeStruct((total, 256), bf16),
+        compiler_params=pltpu.CompilerParams(vmem_limit_bytes=40 * 1024 * 1024),
+        cost_estimate=pl.CostEstimate(
+            flops=1_300_000_000, bytes_accessed=12_000_000, transcendentals=0
+        ),
+        name="late_sums",
+    )(*d_query, *d_key, *d_value, w_query, w_key, table, gain, sums1, sums2, grad)
 
 
 class Moves:
@@ -745,51 +1045,46 @@
     moves = Moves(n_dp, n_mp)
     core = ("dp", 1)
 
-    def all_shares(x):
-        half = x.shape[0] // 2
-        x = lax.dynamic_slice_in_dim(x, moves.core * half, half, 0)[None]
-        shares = [x]
+    def other_shares(x):
+        shares = [x[None]]
         for bit in moves.mp_bits:
             shares = [jnp.concatenate(shares, axis=0)]
             shares.append(moves.swap(shares[0], (bit, bit)))
-        got = jnp.concatenate(shares, axis=0)[1:]
-        other = moves.swap(got, (core, core))
-        first = jnp.where(moves.core == 0, got, other)
-        second = jnp.where(moves.core == 0, other, got)
-        return jnp.concatenate([first, second], axis=1)
-
-    bias_rows = -(-units // width)
-    bias_block = jnp.pad(b_inner, (0, 32 * width - units)).reshape(32, width)
-    far_in = all_shares(w_inner)
-    far_out = all_shares(jnp.concatenate([w_outer, bias_block], axis=0))
-    far_bias = far_out[:, units : units + bias_rows].reshape(n_mp - 1, 1, -1)[:, :, :units]
+        return jnp.concatenate(shares, axis=0)[1:]
+
+    half = units // 2
+    start = moves.core * half
+    half_in = lax.dynamic_slice_in_dim(w_inner, start, half, 1)
+    half_out = lax.dynamic_slice_in_dim(w_outer, start, half, 0)
+    half_bias = jnp.pad(lax.dynamic_slice_in_dim(b_inner, start, half, 0), (0, 16 * width - half))
+    half_out = jnp.concatenate([half_out, half_bias.reshape(16, width)], axis=0)
+    got = (other_shares(half_in), other_shares(half_out))
+    other = tuple(moves.swap(x, (core, core)) for x in got)
 
     line = bucket_line(rows // 2)
     place_ids = np.arange(rows)[None, :]
     forward = jnp.asarray(np.append(line, -1)[:, None] == place_ids).astype(bf16)
     backward = jnp.asarray(np.append(line[::-1], -1)[:, None] == place_ids).astype(bf16)
-    rel_normed, rel_root = ln_parts(wide(rel_table))
-    rel = (rel_normed * wide(rel_gain) + wide(rel_shift)).astype(bf16)
-
-    def project(left, weight, bias):
-        return (dot(left, weight) + wide(bias)).astype(bf16)
-
-    query = project(inputs, w_query, b_query)
-    key = project(inputs, w_key, b_key)
-    value = project(inputs, w_value, b_value)
-    pos_query = project(rel, w_query, b_query)
-    pos_key = project(rel, w_key, b_key)
-    key_line = dot(forward, pos_key).astype(bf16)
-    key_line_back = dot(backward, pos_key).astype(bf16)
-    query_line = dot(backward, pos_query).astype(bf16)
-    bias = jnp.where(valid_pairs(block_group[0], seq_lengths[0], rows), 0.0, -1e30).astype(f32)
-
-    mixed, exps, inverse = attend(query, key, value, key_line, query_line, bias)
-
-    residual = dot(mixed, w_output) + wide(b_output) + wide(inputs)
-    normed1, root1 = ln_parts(residual)
-    hidden_low = (normed1 * wide(norm1_gain) + wide(norm1_shift)).astype(bf16)
-    root1 = jnp.broadcast_to(root1, (rows, TILE))
+    query, key, value, key_line, key_line_back, query_line, both_t = pre(
+        inputs,
+        rel_table,
+        rel_gain,
+        rel_shift,
+        w_query,
+        b_query,
+        w_key,
+        b_key,
+        w_value,
+        b_value,
+        forward,
+        backward,
+    )
+    mixed, exps, inverse = attend(
+        block_group, seq_lengths, query, key, value, key_line, query_line
+    )
+    hidden_low, normed1, root1, part, active, slope = ffn_own(
+        mixed, w_output, b_output, inputs, norm1_gain, norm1_shift, w_inner, b_inner, w_outer
+    )
 
     def far(x):
         whole = x
@@ -798,31 +1093,31 @@
         return whole[rows:]
 
     far_hidden = far(hidden_low)
-    own_in, own_out, own_bias = w_inner[None], w_outer[None], b_inner[None, None]
-    part, active, slope = ffn_own(hidden_low, own_in, own_bias, own_out)
-    zero = jnp.zeros((width,), bf16)
-    vec = jnp.stack(
-        [norm1_gain, norm1_shift, b_outer, norm2_gain, norm2_shift, zero, zero, zero]
-    ).astype(f32)
     far_slope, layer_out, d_pre2, d_branch, sums2 = ffn_rest(
-        hidden_low, far_in, far_bias, far_out, part, normed1, cotangent, vec
+        hidden_low,
+        got,
+        other,
+        part,
+        normed1,
+        cotangent,
+        (norm1_gain, norm1_shift, b_outer, norm2_gain, norm2_shift),
     )
     far_branch = far(d_branch)
-    d_inner, d_residual, d_attn, d_mixed, sums1 = ffn_back(
+    d_inner, d_residual, d_mixed, grad_w_output, sums1 = ffn_back(
         d_branch,
-        own_in,
-        own_out,
+        w_inner,
+        w_outer,
         slope,
-        far_in,
-        far_out,
+        got,
+        other,
         far_slope,
         d_pre2,
         normed1,
         root1,
         w_output,
-        vec,
-    )
-    grad_w_output = dot_tn(mixed, d_attn).astype(bf16)
+        mixed,
+        norm1_gain,
+    )
     ffn = ffn_grads(
         hidden_low,
         d_branch,
@@ -830,78 +1125,55 @@
         d_inner,
         far_hidden,
         far_branch,
-        own_in,
-        own_bias,
-        own_out,
+        w_inner,
+        b_inner,
+        w_outer,
         8 * n_dp,
     )
+    ffn, d_mixed = tie(ffn, d_mixed)
+    ffn = lax.psum(ffn, "dp")
 
     dp_bits, mp_bits = moves.dp_bits, moves.mp_bits
-    turned_bits = dp_bits[1:2] + dp_bits[:1] + dp_bits[2:]
-    ffn_steps = moves.steps(dp_bits, turned_bits)
     first = mp_bits + dp_bits
-    second = dp_bits[1:2] + mp_bits + dp_bits[:1] + dp_bits[2:]
-
-    both = jnp.concatenate([inputs, rel], axis=0)
+    second = dp_bits[:1] + mp_bits + dp_bits[1:]
     cut = 2 * TILE
     groups = width // cut
-    pieces, blocks = [], []
-    early = None
-    for g in range(groups):
-        ffn, d_mixed = tie(ffn, d_mixed)
-        if g == groups - 1:
-            early = jnp.concatenate(
-                [grad_w_output[:, cut * i : cut * (i + 1)] for i in range(groups)] + blocks, axis=0
-            )
-            blocks = []
-            early, d_mixed = tie(early, d_mixed)
-        ffn = ffn_steps.pop(0)(ffn)
-        d_query, d_key, d_value = attend_back(
-            query, key, value, d_mixed, exps, inverse, key_line_back, query_line, backward, 2 * g, 2
-        )
-        pieces.append((d_query, d_key, d_value))
-        blocks.append(dot_tn(both, d_query).astype(bf16))
-        blocks.append(dot_tn(both, d_key).astype(bf16))
-        blocks.append(dot_tn(inputs, d_value).astype(bf16))
+    shared = (exps, inverse, key_line_back, query_line, backward, both_t)
+    dq1, dk1, dv1, grad1 = attend_back(
+        query, key, value, d_mixed, *shared, 0, 2 * (groups - 1)
+    )
+    early = jnp.concatenate([grad_w_output, grad1.reshape(-1, cut)], axis=0)
+    early, d_mixed = tie(early, d_mixed)
     early_steps = moves.steps(first, second)
+    early = early_steps.pop(0)(early)
+    dq2, dk2, dv2, grad2 = attend_back(
+        query, key, value, d_mixed, *shared, 2 * (groups - 1), 2
+    )
+    early, grad2 = tie(early, grad2)
+    early = early_steps.pop(0)(early)
+    late = late_sums(
+        (dq1, dq2),
+        (dk1, dk2),
+        (dv1, dv2),
+        w_query,
+        w_key,
+        rel_table,
+        rel_gain,
+        sums1,
+        sums2,
+        grad2,
+    )
     for step in early_steps:
         early = step(early)
-    for step in ffn_steps:
-        ffn = step(ffn)
-
-    d_query, d_key, d_value = [jnp.concatenate(p, axis=1) for p in zip(*pieces, strict=True)]
-
-    def column_sums(x):
-        return jnp.sum(wide(x), axis=0, keepdims=True)
-
-    back = dot_nt(d_query, w_query) + dot_nt(d_key, w_key)
-    input_grad = d_residual + back[:rows] + dot_nt(d_value, w_value)
-    grad_rel_table, grad_rel_gain, grad_rel_shift = ln_back(
-        back[rows:], rel_normed, rel_root, wide(rel_gain)
-    )
-    vectors = jnp.concatenate(
-        [
-            sums1,
-            sums2,
-            column_sums(d_query),
-            column_sums(d_key),
-            column_sums(d_value),
-            grad_rel_gain,
-            grad_rel_shift,
-            jnp.zeros((11, width), f32),
-        ],
-        axis=0,
-    ).astype(bf16)
-    grad_rel_table = grad_rel_table.astype(bf16)
-    late = jnp.concatenate(
-        blocks
-        + [grad_rel_table[:, cut * i : cut * (i + 1)] for i in range(groups)]
-        + [vectors[:, cut * i : cut * (i + 1)] for i in range(groups)]
-        + [jnp.zeros((256 - 32 * groups, cut), bf16)],
-        axis=0,
-    )
     for step in moves.steps(first, second):
         late = step(late)
+
+    d_query, d_key, d_value = [
+        jnp.concatenate([a[:rows], b[:rows]], axis=1) for a, b in ((dq1, dq2), (dk1, dk2), (dv1, dv2))
+    ]
+    input_grad = (
+        d_residual + dot_nt(d_query, w_query) + dot_nt(d_key, w_key) + dot_nt(d_value, w_value)
+    )
 
     early, late, ffn = wide(early), wide(late), wide(ffn)
 

time: 420 us -> 472 us (1.12)
  waiting for transfers between devices: 102 us -> 181 us
  other arithmetic: 67.1 us -> 34.4 us
  matrix products: 34 us -> 3.83 us
  Pallas kernels: 117 us -> 139 us
  between operations: 3.39 us -> 16.2 us
    psum x0 -> x1, waiting for transfers between devices: none -> 103 us  [per_device(): ffn = lax.psum(ffn, 'dp')]
    ppermute x34 -> x26, waiting for transfers between devices: 102 us -> 78.2 us  [swap(): return lax.ppermute(x, BOTH, perm)]
    dot_general x18 -> x0, matrix products: 23.7 us -> none  [the longest x8 15.6 us: dot(): return jnp.dot(a, b, preferred_element_type=f32)]
    pallas_call x4 -> x6, Pallas kernels: 62.6 us -> 79.1 us  [the longest x1 28.7 us: attend(): pl.pallas_call(attend_kernel, grid=(pairs,), in_specs=[scalars, scalars,...]
    unnamed x198 -> x176, local copies, waits for them, and re-layouts: 31.5 us -> 46.3 us
    select_n x4 -> x0, other arithmetic: 7.49 us -> none  [the longest x2 7.13 us: all_shares(): first = jnp.where(moves.core == 0, got, other)]
    another operation x8 -> x0, local copies, waits for them, and re-layouts: 7.03 us -> none  [per_device(): jnp.stack([norm1_gain, norm1_shift, b_outer, norm2_gain, norm2_shift, zer...]
    dot_general x3, matrix products: 10.4 us -> 3.83 us  [dot_nt(): lax.dot_general(a, b, (((1,), (1,)), ((), ())), preferred_element_type=f32)]
  transfers between devices with their start and end apart: 34 -> 27, of which waited for: 15 -> 15; matrix products, arithmetic and copies ran while one was open for 22% -> 8% of each run, Pallas kernels for 21% -> 20%
where the time goes in v2:
time: 472 us; the launch traced here: 463 us
  waiting for transfers between devices  181 us (38%)
  Pallas kernels  139 us (29%)
  local copies, waits for them, and re-layouts  57.4 us (12%)
  other arithmetic  34.4 us (7%)
  starting transfers between devices  30.4 us (6%)
  between operations  16.2 us (3%)
    psum x1, waiting for transfers between devices, per_device(): ffn = lax.psum(ffn, 'dp')  103 us
    ppermute x26, waiting for transfers between devices, swap(): return lax.ppermute(x, BOTH, perm)  78.2 us
    unnamed x176, local copies, waits for them, and re-layouts  46.3 us
    pallas_call x2, Pallas kernels, attend_back(): pl.pallas_call(attend_back_kernel, grid=(count,), in_specs=[col, col, col...  43.3 us
    ppermute x26, starting transfers between devices, swap(): return lax.ppermute(x, BOTH, perm)  30.3 us
    pallas_call x1, Pallas kernels, attend(): pl.pallas_call(attend_kernel, grid=(pairs,), in_specs=[scalars, scalars,...  28.7 us
    pallas_call x1, Pallas kernels, ffn_back(): pl.pallas_call(functools.partial(ffn_back_kernel, own=own, steps=steps),...  17.5 us
    pallas_call x1, Pallas kernels, ffn_grads(): pl.pallas_call(functools.partial(ffn_grads_kernel, chunks=chunks), grid=(...  17.1 us
  transfers between devices with their start and end apart: 27, of which 15 were waited for; matrix products, arithmetic and copies ran while one was open for 8% of the time, Pallas kernels for 20%

profile of v2, /device:TPU:0, one launch (start us, length us, event | category | flops | bytes accessed | tf_op | source)
XLA Modules:
  0.0 462.6 jit_solution(8810751549141615263)
XLA Ops:
  9.8 3.0 collective-permute-start.1
  18.7 9.6 %pre.1 = (bf16[512,768]{1,0:T(8,128)(2,1)S(1)}, bf16[512,768]{1,0:T(8,128)(2,1)S(1)}, bf16[512,768]{1,0:T(8,128)(2,1)S(1)}, bf16[1024,768]{1,0:T(8,128)(2,1)S(1)...) custom-call(bf16[512,768]{1,0:T(8,128)(2,1)S(1)} %copy-done.40, ...), custom_call_target="tpu_custom_call" | custom-call | flops 5500000256 | bytes 14000000 | tf_op jit(solution)/shard_map/pre/pallas_call | solution.py:136
  30.6 34.0 %collective-permute-done.win_ref.win1_ref = bf16[1,768,768]{2,1,0:T(8,128)(2,1)S(1)} collective-permute-done((bf16[1,768,768]{2,1,0:T(8,128)(2,1)S(1)}, bf16[1,768,768]{2,1,0:T(8,128)(2,1)S(1)}, u32[]{:S(2)}, u32[]{:S(2)}) %collective-permute-start) | collective-permute-done | bytes 1179680 | tf_op jit(solution)/shard_map/ppermute | solution.py:983
  65.1 28.7 %attend.1 = (bf16[512,768]{1,0:T(8,128)(2,1)S(1)}, bf16[12,512,512]{2,1,0:T(8,128)(2,1)S(1)}, f32[6,512,128]{2,1,0:T(8,128)S(1)}) custom-call(s32[1]{0:T(128)S(6)} %copy.47.group_ref, s32[1,4]{1,0:T(1,128)S(1)} %copy-done.50, bf16[512,768]{1,0:T(8,128)(2,1)S(1)} %get-tuple-element.61.q_ref, bf16[512,768]{1,0:T(8,128)(2,1)S(1)} %get-tuple-element.62.k_ref, ...), custom_call_target="tpu_custom_call" | custom-call | flops 17999998976 | bytes 16000000 | tf_op jit(solution)/shard_map/attend/pallas_call | solution.py:251
  93.9 2.7 copy-done.57
  96.7 8.9 %ffn_own.1 = (bf16[512,768]{1,0:T(8,128)(2,1)}, f32[512,768]{1,0:T(8,128)S(1)}, f32[512,128]{1,0:T(8,128)S(1)}, f32[512,768]{1,0:T(8,128)S(1)}, bf16[512,1536]{1...) custom-call(bf16[512,768]{1,0:T(8,128)(2,1)S(1)} %get-tuple-element.66.mixed_ref, bf16[768,768]{1,0:T(8,128)(2,1)S(1)} %copy-done.12, ...), custom_call_target="tpu_custom_call" | custom-call | flops 2415919104 | bytes 14000000 | tf_op jit(solution)/shard_map/ffn_own/pallas_call | solution.py:481
  108.6 11.8 %ffn_rest.1 = (bf16[2,512,768]{2,1,0:T(8,128)(2,1)S(1)}, f32[512,768]{1,0:T(8,128)}, f32[512,768]{1,0:T(8,128)S(1)}, bf16[512,768]{1,0:T(8,128)(2,1)}, f32[8,768]{1,0:T(8,128)S(1)}) custom-call(bf16[512,768]{1,0:T(8,128)(2,1)} %get-tuple-element.67.h_ref, bf16[1,768,768]{2,1,0:T(8,128)(2,1)S(1)} %collective-permute-done.win_ref.win1_ref, ...), custom_call_target="tpu_custom_call" | custom-call | flops 2415919104 | bytes 16000000 | tf_op jit(solution)/shard_map/ffn_rest/pallas_call | solution.py:613
  127.2 17.5 %ffn_back.1 = (bf16[512,1536]{1,0:T(8,128)(2,1)}, f32[512,768]{1,0:T(8,128)}, bf16[512,768]{1,0:T(8,128)(2,1)S(1)}, bf16[2304,256]{1,0:T(8,128)(2,1)S(1)}, f32[8,768]{1,0:T(8,128)S(1)}) custom-call(bf16[512,768]{1,0:T(8,128)(2,1)} %get-tuple-element.71.db_ref, bf16[768,1536]{1,0:T(8,128)(2,1)} %win_ref.5, bf16[1536,768]{1,0:T(8,128)(2,1)} %wout_ref.5, ...), custom_call_target="tpu_custom_call" | custom-call | flops 4831838208 | bytes 22000000 | tf_op jit(solution)/shard_map/ffn_back/pallas_call | solution.py:748
  146.6 17.1 %ffn_grads.1 = bf16[6272,384]{1,0:T(8,128)(2,1)} custom-call(bf16[512,768]{1,0:T(8,128)(2,1)} %get-tuple-element.67.h_ref, bf16[512,768]{1,0:T(8,128)(2,1)} %get-tuple-element.71.db_ref, bf16[512,1536]{1,0:T(8,128)(2,1)S(1)} %copy-done.56, bf16[512,1536]{1,0:T(8,128)(2,1)} %get-tuple-element.78.dinner_ref, ...), custom_call_target="tpu_custom_call" | custom-call | flops 7247757312 | bytes 16000000 | tf_op jit(solution)/shard_map/ffn_grads/pallas_call | solution.py:867
  175.1 28.3 %attend_back.2 = (bf16[1024,512]{1,0:T(8,128)(2,1)S(1)}, bf16[1024,512]{1,0:T(8,128)(2,1)S(1)}, bf16[512,512]{1,0:T(8,128)(2,1)S(1)}, bf16[2,2304,256]{2,1,0:T(8,128)(2,1)}) custom-call(bf16[512,768]{1,0:T(8,128)(2,1)S(1)} %copy-done.71, bf16[512,768]{1,0:T(8,128)(2,1)S(1)} %copy-done.74, bf16[512,768]{1,0:T(8,128)(2,1)S(1)} %copy-done.77, ...), custom_call_target="tpu_custom_call" | custom-call | flops 16000000000 | bytes 12000000 | tf_op jit(solution)/shard_map/attend_back/pallas_call | solution.py:387
  219.7 15.0 %attend_back.3 = (bf16[1024,256]{1,0:T(8,128)(2,1)S(1)}, bf16[1024,256]{1,0:T(8,128)(2,1)S(1)}, bf16[512,256]{1,0:T(8,128)(2,1)S(1)}, bf16[1,2304,256]{2,1,0:T(8,128)(2,1)S(1)}) custom-call(bf16[512,768]{1,0:T(8,128)(2,1)S(1)} %copy-done.72, bf16[512,768]{1,0:T(8,128)(2,1)S(1)} %copy-done.75, bf16[512,768]{1,0:T(8,128)(2,1)S(1)} %copy-done.78, ...), custom_call_target="tpu_custom_call" | custom-call | flops 8000000000 | bytes 6000000 | tf_op jit(solution)/shard_map/attend_back/pallas_call | solution.py:387
  248.7 2.5 late_sums.1
  254.2 102.8 %all-reduce.3.cloned.1.call-done = bf16[6272,384]{1,0:T(8,128)(2,1)} async-done(((bf16[6272,384]{1,0:T(8,128)(2,1)}), bf16[6272,384]{1,0:T(8,128)(2,1)}) %all-reduce.3.cloned.1.call-update) | async-done | bytes 4816912 | tf_op jit(solution)/shard_map/psum | solution.py:1134
  365.9 6.7 %maximum_maximum_fusion = f32[1536,768]{1,0:T(8,128)} fusion(f32[384,384]{1,0:T(8,128)S(1)} %get-tuple-element.128, f32[384,384]{1,0:T(8,128)S(1)} %get-tuple-element.127, f32[384,384]{1,0:T(8,128)S(1)} %get-tuple-element.126, f32[384,384]{1,0:T(8,128)S(1)} %get-tuple-element.125, f32[384,384]{1,0:T(8,128)S(1)} %get-tuple-element.124, ...), kind=kLoop, calls=%fused_computation.1 | loop fusion | flops 8257536 | bytes 9437184 | tf_op jit(solution)/shard_map/concatenate | solution.py:1196
  382.2 2.7 collective-permute-done.9
  385.0 2.7 collective-permute-done.19
  387.8 2.8 collective-permute-start.20
  390.9 6.0 %collective-permute-done.20 = bf16[128,256]{1,0:T(8,128)(2,1)S(1)} collective-permute-done((bf16[128,256]{1,0:T(8,128)(2,1)S(1)}, bf16[128,256]{1,0:T(8,128)(2,1)S(1)}, u32[]{:S(2)}, u32[]{:S(2)}) %collective-permute-start.20) | collective-permute-done | bytes 65568 | tf_op jit(solution)/shard_map/ppermute | solution.py:983
  397.0 3.0 collective-permute-done.10
  402.2 3.6 collective-permute-start.22
  411.5 3.7 collective-permute-done.12
  418.7 9.8 %collective-permute-done.13 = bf16[864,256]{1,0:T(8,128)(2,1)S(1)} collective-permute-done((bf16[864,256]{1,0:T(8,128)(2,1)S(1)}, bf16[864,256]{1,0:T(8,128)(2,1)S(1)}, u32[]{:S(2)}, u32[]{:S(2)}) %collective-permute-start.13) | collective-permute-done | bytes 442400 | tf_op jit(solution)/shard_map/ppermute | solution.py:983
  431.7 2.8 pad_maximum_fusion
  435.1 7.9 %collective-permute-done.14 = bf16[1728,256]{1,0:T(8,128)(2,1)} collective-permute-done((bf16[1728,256]{1,0:T(8,128)(2,1)}, bf16[1728,256]{1,0:T(8,128)(2,1)}, u32[]{:S(2)}, u32[]{:S(2)}) %collective-permute-start.14) | collective-permute-done | bytes 884768 | tf_op jit(solution)/shard_map/ppermute | solution.py:983
  (287 shorter events, 112.8 us)
Async XLA Ops:
  7.2 349.8 %all-reduce.3.cloned.1.call-start = ((), (), s32[]{:S(2)}) async-start(), calls=%async_computation | async-start | bytes 9633792 | tf_op jit(solution)/shard_map/psum | solution.py:1134
  9.8 54.8 %collective-permute-start.1 = (bf16[1,784,768]{2,1,0:T(8,128)(2,1)S(1)}, bf16[1,784,768]{2,1,0:T(8,128)(2,1)S(1)}, u32[]{:S(2)}, u32[]{:S(2)}) collective-permute-start(bf16[1,784,768]{2,1,0:T(8,128)(2,1)S(1)} %maximum_bitcast_fusion), channel_id=1, source_target_pairs={{0,1},{1,0},{2,3},{3,2},{4,5},{5,4},{6,7},{7,6},{8,9},{9,8},{10,11... | collective-permute-start | bytes 3612680 | tf_op jit(solution)/shard_map/ppermute | solution.py:983
  12.9 51.7 %collective-permute-start = (bf16[1,768,768]{2,1,0:T(8,128)(2,1)S(1)}, bf16[1,768,768]{2,1,0:T(8,128)(2,1)S(1)}, u32[]{:S(2)}, u32[]{:S(2)}) collective-permute-start(bf16[1,768,768]{2,1,0:T(8,128)(2,1)S(1)} %dynamic-slice_bitcast_fusion), channel_id=1, source_target_pairs={{0,1},{1,0},{2,3},{3,2},{4,5},{5,4},{6,7},{7,6},{8,9},{9,8},{10,11... | collective-permute-start | bytes 3538952 | tf_op jit(solution)/shard_map/ppermute | solution.py:983
  64.6 44.0 %collective-permute-start.2 = (bf16[1,768,768]{2,1,0:T(8,128)(2,1)S(1)}, bf16[1,768,768]{2,1,0:T(8,128)(2,1)S(1)}, u32[]{:S(2)}, u32[]{:S(2)}) collective-permute-start(bf16[1,768,768]{2,1,0:T(8,128)(2,1)S(1)} %collective-permute-done.win_ref.win1_ref), channel_id=1, source_target_pairs={{0,2},{1,3},{2,0},{3,1},{4,6},{5,7},{6,4},{7,5},{8,10},{9,11},{10,... | collective-permute-start | bytes 3538952 | tf_op jit(solution)/shard_map/ppermute | solution.py:983
  64.6 44.0 %collective-permute-start.3 = (bf16[1,784,768]{2,1,0:T(8,128)(2,1)S(1)}, bf16[1,784,768]{2,1,0:T(8,128)(2,1)S(1)}, u32[]{:S(2)}, u32[]{:S(2)}) collective-permute-start(bf16[1,784,768]{2,1,0:T(8,128)(2,1)S(1)} %collective-permute-done.1.bin_ref.wout_ref.wout1_ref), channel_id=1, source_target_pairs={{0,2},{1,3},{2,0},{3,1},{4,6},{5,7},{6,4},{7,5},{8,10},{9,11},{10,... | collective-permute-start | bytes 3612680 | tf_op jit(solution)/shard_map/ppermute | solution.py:983
  106.8 39.8 %collective-permute-start.4 = (bf16[512,768]{1,0:T(8,128)(2,1)}, bf16[512,768]{1,0:T(8,128)(2,1)}, u32[]{:S(2)}, u32[]{:S(2)}) collective-permute-start(bf16[512,768]{1,0:T(8,128)(2,1)} %get-tuple-element.67.h_ref), channel_id=1, source_target_pairs={{0,1},{1,0},{2,3},{3,2},{4,5},{5,4},{6,7},{7,6},{8,9},{9,8},{10,11... | collective-permute-start | bytes 2359304 | tf_op jit(solution)/shard_map/ppermute | solution.py:983
  122.7 23.9 %collective-permute-start.5 = (bf16[512,768]{1,0:T(8,128)(2,1)}, bf16[512,768]{1,0:T(8,128)(2,1)}, u32[]{:S(2)}, u32[]{:S(2)}) collective-permute-start(bf16[512,768]{1,0:T(8,128)(2,1)} %get-tuple-element.71.db_ref), channel_id=1, source_target_pairs={{0,1},{1,0},{2,3},{3,2},{4,5},{5,4},{6,7},{7,6},{8,9},{9,8},{10,11... | collective-permute-start | bytes 2359304 | tf_op jit(solution)/shard_map/ppermute | solution.py:983
  208.3 34.4 %collective-permute-start.6 = (bf16[3456,256]{1,0:T(8,128)(2,1)}, bf16[3456,256]{1,0:T(8,128)(2,1)}, u32[]{:S(2)}, u32[]{:S(2)}) collective-permute-start(bf16[3456,256]{1,0:T(8,128)(2,1)} %constant_dynamic-slice_fusion.9), channel_id=1, source_target_pairs={{0,2},{1,3},{2,0},{3,1},{4,6},{5,7},{6,4},{7,5},{8,10},{9,11},{10,... | collective-permute-start | bytes 5308424 | tf_op jit(solution)/shard_map/ppermute | solution.py:983
  247.1 112.0 %collective-permute-start.7 = (bf16[1728,256]{1,0:T(8,128)(2,1)}, bf16[1728,256]{1,0:T(8,128)(2,1)}, u32[]{:S(2)}, u32[]{:S(2)}) collective-permute-start(bf16[1728,256]{1,0:T(8,128)(2,1)} %constant_dynamic-slice_fusion.8), channel_id=1, source_target_pairs={{0,1},{1,0},{2,6},{3,7},{4,5},{5,4},{6,2},{7,3},{8,9},{9,8},{10,14... | collective-permute-start | bytes 2654216 | tf_op jit(solution)/shard_map/ppermute | solution.py:983
  251.4 111.5 %collective-permute-start.16 = (bf16[2048,256]{1,0:T(8,128)(2,1)S(1)}, bf16[2048,256]{1,0:T(8,128)(2,1)}, u32[]{:S(2)}, u32[]{:S(2)}) collective-permute-start(bf16[2048,256]{1,0:T(8,128)(2,1)S(1)} %constant_dynamic-slice_fusion.4), channel_id=1, source_target_pairs={{0,2},{1,3},{2,0},{3,1},{4,6},{5,7},{6,4},{7,5},{8,10},{9,11},{10,... | collective-permute-start | bytes 3145736 | tf_op jit(solution)/shard_map/ppermute | solution.py:983
  361.4 14.2 %collective-permute-start.8 = (bf16[864,256]{1,0:T(8,128)(2,1)}, bf16[864,256]{1,0:T(8,128)(2,1)}, u32[]{:S(2)}, u32[]{:S(2)}) collective-permute-start(bf16[864,256]{1,0:T(8,128)(2,1)} %constant_dynamic-slice_fusion.7), channel_id=1, source_target_pairs={{0,4},{1,5},{2,3},{3,2},{4,0},{5,1},{6,7},{7,6},{8,12},{9,13},{10,... | collective-permute-start | bytes 1327112 | tf_op jit(solution)/shard_map/ppermute | solution.py:983
  364.4 9.4 %collective-permute-start.17 = (bf16[1024,256]{1,0:T(8,128)(2,1)S(1)}, bf16[1024,256]{1,0:T(8,128)(2,1)S(1)}, u32[]{:S(2)}, u32[]{:S(2)}) collective-permute-start(bf16[1024,256]{1,0:T(8,128)(2,1)S(1)} %constant_dynamic-slice_fusion.3), channel_id=1, source_target_pairs={{0,1},{1,0},{2,6},{3,7},{4,5},{5,4},{6,2},{7,3},{8,9},{9,8},{10,14... | collective-permute-start | bytes 1572872 | tf_op jit(solution)/shard_map/ppermute | solution.py:983
  376.8 8.1 %collective-permute-start.9 = (bf16[432,256]{1,0:T(8,128)(2,1)S(1)}, bf16[432,256]{1,0:T(8,128)(2,1)S(1)}, u32[]{:S(2)}, u32[]{:S(2)}) collective-permute-start(bf16[432,256]{1,0:T(8,128)(2,1)S(1)} %constant_dynamic-slice_fusion.6), channel_id=1, source_target_pairs={{0,8},{1,9},{2,10},{3,11},{4,12},{5,13},{6,14},{7,15},{8,0},{9,1},... | collective-permute-start | bytes 663560 | tf_op jit(solution)/shard_map/ppermute | solution.py:983
  380.6 7.2 %collective-permute-start.19 = (bf16[256,256]{1,0:T(8,128)(2,1)S(1)}, bf16[256,256]{1,0:T(8,128)(2,1)S(1)}, u32[]{:S(2)}, u32[]{:S(2)}) collective-permute-start(bf16[256,256]{1,0:T(8,128)(2,1)S(1)} %constant_dynamic-slice_fusion.1), channel_id=1, source_target_pairs={{0,8},{1,9},{2,10},{3,11},{4,12},{5,13},{6,14},{7,15},{8,0},{9,1},... | collective-permute-start | bytes 393224 | tf_op jit(solution)/shard_map/ppermute | solution.py:983
  387.8 9.1 %collective-permute-start.20 = (bf16[128,256]{1,0:T(8,128)(2,1)S(1)}, bf16[128,256]{1,0:T(8,128)(2,1)S(1)}, u32[]{:S(2)}, u32[]{:S(2)}) collective-permute-start(bf16[128,256]{1,0:T(8,128)(2,1)S(1)} %constant_dynamic-slice_fusion), channel_id=1, source_target_pairs={{0,16},{1,17},{2,18},{3,19},{4,20},{5,21},{6,22},{7,23},{8,24},{9,... | collective-permute-start | bytes 196616 | tf_op jit(solution)/shard_map/ppermute | solution.py:983
  390.6 9.4 %collective-permute-start.10 = (bf16[216,256]{1,0:T(8,128)(2,1)S(1)}, bf16[216,256]{1,0:T(8,128)(2,1)S(1)}, u32[]{:S(2)}, u32[]{:S(2)}) collective-permute-start(bf16[216,256]{1,0:T(8,128)(2,1)S(1)} %constant_dynamic-slice_fusion.5), channel_id=1, source_target_pairs={{0,16},{1,17},{2,18},{3,19},{4,20},{5,21},{6,22},{7,23},{8,24},{9,... | collective-permute-start | bytes 331784 | tf_op jit(solution)/shard_map/ppermute | solution.py:983
  400.0 7.9 %collective-permute-start.11 = (bf16[216,256]{1,0:T(8,128)(2,1)S(1)}, bf16[216,256]{1,0:T(8,128)(2,1)S(1)}, u32[]{:S(2)}, u32[]{:S(2)}) collective-permute-start(bf16[216,256]{1,0:T(8,128)(2,1)S(1)} %add_convert_fusion.8), channel_id=1, source_target_pairs={{0,16},{1,17},{2,18},{3,19},{4,20},{5,21},{6,22},{7,23},{8,24},{9,... | collective-permute-start | bytes 331784 | tf_op jit(solution)/shard_map/ppermute | solution.py:983
  402.2 6.9 %collective-permute-start.22 = (bf16[256,256]{1,0:T(8,128)(2,1)S(1)}, bf16[256,256]{1,0:T(8,128)(2,1)S(1)}, u32[]{:S(2)}, u32[]{:S(2)}) collective-permute-start(bf16[256,256]{1,0:T(8,128)(2,1)S(1)} %pad_maximum_fusion.14), channel_id=1, source_target_pairs={{0,8},{1,9},{2,10},{3,11},{4,12},{5,13},{6,14},{7,15},{8,0},{9,1},... | collective-permute-start | bytes 393224 | tf_op jit(solution)/shard_map/ppermute | solution.py:983
  408.0 7.2 %collective-permute-start.12 = (bf16[432,256]{1,0:T(8,128)(2,1)S(1)}, bf16[432,256]{1,0:T(8,128)(2,1)S(1)}, u32[]{:S(2)}, u32[]{:S(2)}) collective-permute-start(bf16[432,256]{1,0:T(8,128)(2,1)S(1)} %pad_maximum_fusion.13), channel_id=1, source_target_pairs={{0,8},{1,9},{2,10},{3,11},{4,12},{5,13},{6,14},{7,15},{8,0},{9,1},... | collective-permute-start | bytes 663560 | tf_op jit(solution)/shard_map/ppermute | solution.py:983
  409.2 7.5 %collective-permute-start.23 = (bf16[512,256]{1,0:T(8,128)(2,1)S(1)}, bf16[512,256]{1,0:T(8,128)(2,1)S(1)}, u32[]{:S(2)}, u32[]{:S(2)}) collective-permute-start(bf16[512,256]{1,0:T(8,128)(2,1)S(1)} %pad_maximum_fusion.12), channel_id=1, source_target_pairs={{0,4},{1,5},{2,3},{3,2},{4,0},{5,1},{6,7},{7,6},{8,12},{9,13},{10,... | collective-permute-start | bytes 786440 | tf_op jit(solution)/shard_map/ppermute | solution.py:983
  415.4 13.1 %collective-permute-start.13 = (bf16[864,256]{1,0:T(8,128)(2,1)S(1)}, bf16[864,256]{1,0:T(8,128)(2,1)S(1)}, u32[]{:S(2)}, u32[]{:S(2)}) collective-permute-start(bf16[864,256]{1,0:T(8,128)(2,1)S(1)} %pad_maximum_fusion.11), channel_id=1, source_target_pairs={{0,4},{1,5},{2,3},{3,2},{4,0},{5,1},{6,7},{7,6},{8,12},{9,13},{10,... | collective-permute-start | bytes 1327112 | tf_op jit(solution)/shard_map/ppermute | solution.py:983
  416.9 13.6 %collective-permute-start.24 = (bf16[1024,256]{1,0:T(8,128)(2,1)S(1)}, bf16[1024,256]{1,0:T(8,128)(2,1)S(1)}, u32[]{:S(2)}, u32[]{:S(2)}) collective-permute-start(bf16[1024,256]{1,0:T(8,128)(2,1)S(1)} %pad_maximum_fusion.10), channel_id=1, source_target_pairs={{0,1},{1,0},{2,6},{3,7},{4,5},{5,4},{6,2},{7,3},{8,9},{9,8},{10,14... | collective-permute-start | bytes 1572872 | tf_op jit(solution)/shard_map/ppermute | solution.py:983
  429.7 13.4 %collective-permute-start.14 = (bf16[1728,256]{1,0:T(8,128)(2,1)}, bf16[1728,256]{1,0:T(8,128)(2,1)}, u32[]{:S(2)}, u32[]{:S(2)}) collective-permute-start(bf16[1728,256]{1,0:T(8,128)(2,1)} %pad_maximum_fusion.9), channel_id=1, source_target_pairs={{0,1},{1,0},{2,6},{3,7},{4,5},{5,4},{6,2},{7,3},{8,9},{9,8},{10,14... | collective-permute-start | bytes 2654216 | tf_op jit(solution)/shard_map/ppermute | solution.py:983
  431.7 13.0 %collective-permute-start.25 = (bf16[2048,256]{1,0:T(8,128)(2,1)}, bf16[2048,256]{1,0:T(8,128)(2,1)S(1)}, u32[]{:S(2)}, u32[]{:S(2)}) collective-permute-start(bf16[2048,256]{1,0:T(8,128)(2,1)} %pad_maximum_fusion.8), channel_id=1, source_target_pairs={{0,2},{1,3},{2,0},{3,1},{4,6},{5,7},{6,4},{7,5},{8,10},{9,11},{10,... | collective-permute-start | bytes 3145736 | tf_op jit(solution)/shard_map/ppermute | solution.py:983
  (91 other events, 1006.0 us)
Sparse Core Ops, SparseCore 0:
  237.4 119.5 all-reduce.2
